TPU v7x, 32 devices: a whole 2x2x4 slice. The times are simulated.
32 devices in a mesh: row: 8 (over y, x, core), col: 4 (over z).
Axes of the slice: x: 2, y: 2, z: 4, core: 2. Of those that a mesh axis runs over, the one named last changes fastest.
Arguments:
- p_cols: int32 [128, 16], P('row', 'col'), may hold values from -1 to 31, as said below
- p_data: float32 [8192, 1024], P('row', 'col'), may hold values from -1.5 to 1.5
Outputs:
- product: float32 [8192, 8192], P('row', 'col')
Inputs may be any that keep to these rules, and one draw needn't show every extreme that they name: `p_cols`: in each column tile, each block row has 1 to 4 used slots, the used ones first, with distinct columns; the first block row of each device's rows has all 4 used.
All inputs are finite; a program needn't handle non-finite values.
Results may differ from a plain program's by a relative error of at most 0.0003.
Values sent between devices are 32-bit elements; how exact they have to be, the bound alone decides.
No kernel may reach another device: no remote copies, remote signals or barrier semaphores. Data moves between devices by JAX's collectives and lax.ppermute only.
A program may use at most 192 MiB of HBM per device.

v0:
```python
import functools

import jax
import jax.numpy as jnp
import numpy as np
from jax import lax
from jax.experimental import pallas as pl
from jax.experimental.pallas import tpu as pltpu
from jax.sharding import PartitionSpec as P

BS = 64
STEPS = 4
UNROLL = 4
EXTRA = 8


def left_offsets(row, ratio, n_col):
    seen = []
    for step in range(STEPS):
        offset = (row + step) // ratio % n_col
        if offset not in seen:
            seen.append(offset)
    return seen


def shift(rows, step, count):
    return [((r, c), (r, (c + step) % count)) for r in rows for c in range(count)]


def left_plan(n_row, n_col, ratio):
    offsets = [left_offsets(row, ratio, n_col) for row in range(n_row)]
    if (n_row, n_col, ratio) != (8, 4, 2):
        perms = []
        for slot in range(max(len(o) for o in offsets)):
            pairs = [
                ((row, (col + offsets[row][slot]) % n_col), (row, col))
                for row in range(n_row)
                for col in range(n_col)
                if slot < len(offsets[row]) and offsets[row][slot] != 0
            ]
            perms.append((0, pairs))
        return perms
    down = shift([r for r in range(8) if 1 in offsets[r]], -1, 4)
    up = shift([r for r in range(8) if 3 in offsets[r]], 1, 4)
    again_down = shift([r for r in range(8) if {1, 2} <= set(offsets[r]) and 3 not in offsets[r]], -1, 4)
    again_up = shift([r for r in range(8) if {2, 3} <= set(offsets[r]) and 1 not in offsets[r]], 1, 4)
    for r in range(8):
        if {1, 2, 3} <= set(offsets[r]):
            again_down += [((r, 1), (r, 0)), ((r, 2), (r, 1))]
            again_up += [((r, 1), (r, 2)), ((r, 2), (r, 3))]
    return [(0, down), (0, up), (1, again_down), (2, again_up)]


def right_plan(n_row, n_col, ratio):
    everyone = [(row, col) for row in range(n_row) for col in range(n_col)]
    if (n_row, n_col, ratio) != (8, 4, 2):
        return [
            (0, [(((r + ratio * c + step) % n_row, c), (r, c)) for r, c in everyone if (ratio * c + step) % n_row])
            for step in range(STEPS)
        ]
    first = [(((r + 2 * c) % 8, c), (r, c)) for r, c in everyone if c != 0]
    first += [((r + 1, 0), (r, 0)) for r in range(0, 8, 2)]
    second = [(((r + 2 * c + 2) % 8, c), (r, c)) for r, c in everyone if c != 3]
    second += [((r ^ 1, 3), (r, 3)) for r in range(8)]
    last = [(((r - 1 + 2 * c + 4) % 8, c), (r, c)) for r, c in everyone if r % 2 == 1]
    first_swap = [((r + 1, c), (r, c)) for r, c in everyone if r % 2 == 0 and c != 0]
    second_swap = [((r ^ 1, c), (r, c)) for r, c in everyone if c != 3]
    return [(0, first), (0, second), (0, last), (1, first_swap), (2, second_swap)]


def carry_out(perms, n_row, n_col):
    held = [{(r, c): (r, c) for r in range(n_row) for c in range(n_col)}]
    for source, pairs in perms:
        held.append({dst: held[source][src] for src, dst in pairs})
    return held


def device_table(left_perms, right_perms, n_row, n_col, ratio):
    left_held = carry_out(left_perms, n_row, n_col)
    right_held = carry_out(right_perms, n_row, n_col)
    slots = (ratio - 1 + STEPS - 1) // ratio + 1
    table = np.full((n_row, n_col, 2 * slots + STEPS), -1, np.int32)

    def find(held, device, tile):
        return [i for i, h in enumerate(held) if h.get(device) == tile][0]

    for r in range(n_row):
        for c in range(n_col):
            for slot, offset in enumerate(left_offsets(r, ratio, n_col)):
                tile_col = (c + offset) % n_col
                table[r, c, slot] = find(left_held, (r, c), (r, tile_col))
                table[r, c, slots + STEPS + slot] = (tile_col * ratio - r - ratio * c) % n_row
            for step in range(STEPS):
                table[r, c, slots + step] = find(right_held, (r, c), ((r + ratio * c + step) % n_row, c))
    return table, slots


def fetch(choice, bufs, target, sem):
    for number, buf in enumerate(bufs):
        @pl.when(choice == number)
        def _():
            pltpu.make_async_copy(buf, target, sem).start()


def split_kernel(slots, rb, info_ref, *refs):
    bufs, (split_ref, code_ref), (raw, sem) = refs[:-4], refs[-4:-2], refs[-2:]
    rows = raw.shape[1] - EXTRA
    for step in range(STEPS):
        fetch(info_ref[slots + step], bufs, raw.at[step], sem.at[step])
    code_ref[...] = jnp.full(code_ref.shape, 2 << 16, jnp.int32)
    for step in range(STEPS):
        pltpu.make_async_copy(bufs[0], raw.at[step], sem.at[step]).wait()
        col = raw[step, rows : rows + 1, 0 : code_ref.shape[1]].astype(jnp.int32)
        code = (col >> 1) * 2 * BS | (col & 1) << 16
        code_ref[step : step + 1, :] = jnp.where(col < 0, 2 << 16, code)

        @pl.loop(0, rb)
        def _(block):
            x = raw[step, pl.ds(pl.multiple_of(block * BS, BS), BS), :]
            hi = x.astype(jnp.bfloat16)
            split_ref[step * rb + block, 0:BS, :] = hi
            split_ref[step * rb + block, BS : 2 * BS, :] = (x - hi.astype(jnp.float32)).astype(jnp.bfloat16)


def list_kernel(slots, n_row, rb, w, ratio, info_ref, *refs):
    bufs, code_ref, (cols, sem) = refs[:-3], refs[-3], refs[-2:]
    rows = bufs[0].shape[0] - EXTRA
    for slot in range(slots):
        fetch(info_ref[slot], [buf.at[pl.ds(rows, EXTRA)] for buf in bufs], cols.at[slot], sem.at[slot])
    place = lax.broadcasted_iota(jnp.int32, (1, code_ref.shape[1]), 1)
    for slot in range(slots):
        used = info_ref[slot] >= 0

        @pl.when(used)
        def _():
            pltpu.make_async_copy(bufs[0].at[pl.ds(rows, EXTRA)], cols.at[slot], sem.at[slot]).wait()

        inner = cols[slot, 0:1, 0 : code_ref.shape[1]].astype(jnp.int32)
        valid = (inner >= 0) & (place < rb * w)
        step = jnp.full(inner.shape, info_ref[slots + STEPS + slot], jnp.int32)
        for _ in range(ratio - 1):
            beyond = inner >= rb
            step = jnp.where(beyond, step + 1, step)
            inner = jnp.where(beyond, inner - rb, inner)
        step = jnp.where(step >= n_row, step - n_row, step)
        code = (step * rb + inner) | (place & (w - 1)) << 8 | slot << 12 | (place // w) << 16
        valid = valid & (step < STEPS)
        code_ref[slot : slot + 1, :] = jnp.where(valid, jnp.where(used, code, -1), -1)


def product_kernel(slots, rb, w, info_ref, lcode_ref, rcode_ref, split_ref, *refs):
    bufs, out_ref = refs[:-6], refs[-6]
    left, acc, codes, sem, osem = refs[-5:]
    rows, width = left.shape[1] - EXTRA, left.shape[2]
    for slot in range(slots):
        fetch(info_ref[slot], bufs, left.at[slot], sem.at[slot])

    @pl.loop(0, rb)
    def _(r):
        acc[pl.ds(pl.multiple_of(r * BS, BS), BS), :] = jnp.zeros((BS, acc.shape[1]), jnp.float32)

    for slot in range(slots):
        @pl.when(info_ref[slot] >= 0)
        def _():
            pltpu.make_async_copy(bufs[0], left.at[slot], sem.at[slot]).wait()

    part_rows = rb // STEPS
    bounds = [0]
    for part in range(STEPS):
        def listed(i, place):
            for slot in range(slots):
                for k in range(w):
                    code = lcode_ref[slot, (part * part_rows + i) * w + k]
                    codes[place] = code
                    place = place + (code >= 0).astype(jnp.int32)
            return place

        end = lax.fori_loop(0, part_rows, listed, bounds[-1])
        for u in range(UNROLL - 1):
            codes[end + u] = STEPS * rb
        bounds.append((end + UNROLL - 1) // UNROLL * UNROLL)

    low = lax.broadcasted_iota(jnp.int32, (BS, 2 * BS), 1) < BS
    half = lax.broadcasted_iota(jnp.int32, (BS, 2 * BS), 1) // BS

    def product(code):
        block = code & 255
        slot = (code >> 8) & 15
        tile = (code >> 12) & 15
        row = (code >> 16) * BS
        x = left[tile, pl.ds(pl.multiple_of(row, BS), BS), pl.ds(pl.multiple_of((slot >> 1) * 2 * BS, 2 * BS), 2 * BS)]
        both = jnp.where(half == (slot & 1), x, pltpu.roll(x, BS, 1))
        hi = both.astype(jnp.bfloat16).astype(jnp.float32)
        lhs = jnp.where(low, hi, both - hi).astype(jnp.bfloat16)
        lhs = jnp.concatenate([lhs, lhs], axis=1)
        hi, lo = split_ref[block, 0:BS, :], split_ref[block, BS : 2 * BS, :]
        rhs = jnp.concatenate([hi, hi, lo, lo], axis=0)
        return block, row, jnp.dot(lhs, rhs, preferred_element_type=jnp.float32)

    def add(block, row, value):
        step = block // rb
        inner = (block - step * rb) * w
        for pair in range(w // 2):
            x = value[:, pair * 2 * BS : (pair + 1) * 2 * BS]
            turned = pltpu.roll(x, BS, 1)
            for side in range(2):
                code = rcode_ref[step, inner + 2 * pair + side]
                parity = code >> 16
                picked = jnp.where(parity == side, x, turned)
                picked = jnp.where(half == parity, picked, 0.0)
                base = pl.multiple_of(code & 0xFFFF, 2 * BS)
                acc[pl.ds(pl.multiple_of(row, BS), BS), pl.ds(base, 2 * BS)] += picked

    def out_copy(part):
        at = pl.ds(part * part_rows * BS, part_rows * BS)
        return pltpu.make_async_copy(acc.at[at], out_ref.at[at], osem.at[part])

    for part in range(STEPS):
        @pl.loop(bounds[part] // UNROLL, bounds[part + 1] // UNROLL)
        def _(group):
            done = [product(codes[group * UNROLL + u]) for u in range(UNROLL)]
            for item in done:
                add(*item)

        out_copy(part).start()
    for part in range(STEPS):
        out_copy(part).wait()


def local(p_cols, p_data):
    n_row, n_col = lax.axis_size("row"), lax.axis_size("col")
    ratio = n_row // n_col
    row_id, col_id = lax.axis_index("row"), lax.axis_index("col")
    rb, w = p_cols.shape
    rows, width = p_data.shape
    left_perms = left_plan(n_row, n_col, ratio)
    right_perms = right_plan(n_row, n_col, ratio)
    table, slots = device_table(left_perms, right_perms, n_row, n_col, ratio)
    info = jnp.asarray(table)[row_id, col_id]

    cols = jnp.pad(p_cols.astype(jnp.float32).reshape(1, -1), ((0, EXTRA - 1), (0, width - rb * w)))
    own = jnp.concatenate([p_data, cols], axis=0)

    def permute(value, pairs):
        return lax.ppermute(value, ("row", "col"), [(s[0] * n_col + s[1], d[0] * n_col + d[1]) for s, d in pairs])

    left_bufs, right_bufs = [own], [own]
    for source, pairs in left_perms:
        left_bufs.append(permute(left_bufs[source], pairs))
    for source, pairs in right_perms:
        right_bufs.append(permute(right_bufs[source], pairs))
    smem = pl.BlockSpec(memory_space=pltpu.SMEM)
    vmem = pl.BlockSpec(memory_space=pltpu.VMEM)
    hbm = pl.BlockSpec(memory_space=pl.ANY)
    dma = pltpu.SemaphoreType.DMA
    split, rcode = pl.pallas_call(
        functools.partial(split_kernel, slots, rb),
        out_shape=(
            jax.ShapeDtypeStruct((STEPS * rb + 1, 2 * BS, width), jnp.bfloat16),
            jax.ShapeDtypeStruct((8, 128), jnp.int32),
        ),
        in_specs=[smem] + [hbm] * len(right_bufs),
        out_specs=(vmem, vmem),
        scratch_shapes=[pltpu.VMEM((STEPS, rows + EXTRA, width), jnp.float32), dma((STEPS,))],
        compiler_params=pltpu.CompilerParams(vmem_limit_bytes=16 << 20),
        cost_estimate=pl.CostEstimate(flops=10**7, bytes_accessed=8 << 20, transcendentals=0),
    )(info, *right_bufs)
    out_shape = jax.ShapeDtypeStruct((rows, rb * ratio * BS), jnp.float32)
    lcode = pl.pallas_call(
        functools.partial(list_kernel, slots, n_row, rb, w, ratio),
        out_shape=jax.ShapeDtypeStruct((8, 128), jnp.int32),
        in_specs=[smem] + [hbm] * len(left_bufs),
        out_specs=vmem,
        scratch_shapes=[pltpu.VMEM((slots, EXTRA, width), jnp.float32), dma((slots,))],
        compiler_params=pltpu.CompilerParams(vmem_limit_bytes=4 << 20),
        cost_estimate=pl.CostEstimate(flops=10**11, bytes_accessed=1 << 20, transcendentals=0),
    )(info, *left_bufs)
    return pl.pallas_call(
        functools.partial(product_kernel, slots, rb, w),
        out_shape=out_shape,
        in_specs=[smem, smem, smem, vmem] + [hbm] * len(left_bufs),
        out_specs=hbm,
        scratch_shapes=[
            pltpu.VMEM((slots, rows + EXTRA, width), jnp.float32),
            pltpu.VMEM(out_shape.shape, jnp.float32),
            pltpu.SMEM((slots * rb * w + STEPS * UNROLL,), jnp.int32),
            dma((slots,)),
            dma((STEPS,)),
        ],
        compiler_params=pltpu.CompilerParams(vmem_limit_bytes=24 << 20),
        cost_estimate=pl.CostEstimate(flops=10**9, bytes_accessed=20 << 20, transcendentals=0),
    )(info, lcode, rcode, split, *left_bufs)


def solution(mesh):
    in_specs = (P("row", "col"), P("row", "col"))
    return jax.shard_map(local, mesh=mesh, in_specs=in_specs, out_specs=P("row", "col"), check_vma=False)
```

profile of v0, /device:TPU:11, one launch (start us, length us, event | category | flops | bytes accessed | tf_op | source)
XLA Modules:
  0.0 87.9 jit_solution(4358567427607592136)
XLA Ops:
  0.0 0.7 convert_element_type.5
  0.7 0.1 copy.5
  0.8 0.1 reshape.3
  0.9 1.3 %select_maximum_fusion.refs_0_ = f32[1032,256]{1,0:T(8,128)S(1)} fusion(f32[1,64]{1,0:T(1,128)S(1)} %reshape.3, f32[1024,256]{1,0:T(8,128)} %param.4), kind=kLoop, calls=%fused_computation | loop fusion | flops 792576 | bytes 2105600 | tf_op jit(solution)/shard_map/concatenate | solution.py:242
  2.2 3.2 %collective-permute-start.1 = (f32[1032,256]{1,0:T(8,128)S(1)}, f32[1032,256]{1,0:T(8,128)S(1)}, u32[]{:S(2)}, u32[]{:S(2)}) collective-permute-start(f32[1032,256]{1,0:T(8,128)S(1)} %select_maximum_fusion.refs_0_), channel_id=1, source_target_pairs={{12,13},{13,14},{14,15},{15,12},{16,17},{17,18},{18,19},{19,16},{2... | collective-permute-start | bytes 3170312 | tf_op jit(solution)/shard_map/ppermute | solution.py:245
  5.4 2.1 %collective-permute-start = (f32[1032,256]{1,0:T(8,128)S(1)}, f32[1032,256]{1,0:T(8,128)S(1)}, u32[]{:S(2)}, u32[]{:S(2)}) collective-permute-start(f32[1032,256]{1,0:T(8,128)S(1)} %select_maximum_fusion.refs_0_), channel_id=1, source_target_pairs={{0,3},{1,0},{2,1},{3,2},{4,7},{5,4},{6,5},{7,6},{8,11},{9,8},{10,9... | collective-permute-start | bytes 3170312 | tf_op jit(solution)/shard_map/ppermute | solution.py:245
  7.5 1.3 %collective-permute-start.5 = (f32[1032,256]{1,0:T(8,128)S(1)}, f32[1032,256]{1,0:T(8,128)}, u32[]{:S(2)}, u32[]{:S(2)}) collective-permute-start(f32[1032,256]{1,0:T(8,128)S(1)} %select_maximum_fusion.refs_0_), channel_id=1, source_target_pairs={{8,0},{17,1},{26,2},{12,4},{21,5},{30,6},{16,8},{25,9},{2,10},{20,... | collective-permute-start | bytes 3170312 | tf_op jit(solution)/shard_map/ppermute | solution.py:245
  8.7 1.9 %collective-permute-start.4 = (f32[1032,256]{1,0:T(8,128)S(1)}, f32[1032,256]{1,0:T(8,128)}, u32[]{:S(2)}, u32[]{:S(2)}) collective-permute-start(f32[1032,256]{1,0:T(8,128)S(1)} %select_maximum_fusion.refs_0_), channel_id=1, source_target_pairs={{9,1},{18,2},{27,3},{13,5},{22,6},{31,7},{17,9},{26,10},{3,11},{21... | collective-permute-start | bytes 3170312 | tf_op jit(solution)/shard_map/ppermute | solution.py:245
  10.7 14.9 %collective-permute-done.1.refs_2_ = f32[1032,256]{1,0:T(8,128)S(1)} collective-permute-done((f32[1032,256]{1,0:T(8,128)S(1)}, f32[1032,256]{1,0:T(8,128)S(1)}, u32[]{:S(2)}, u32[]{:S(2)}) %collective-permute-start.1) | collective-permute-done | bytes 1056800 | tf_op jit(solution)/shard_map/ppermute | solution.py:245
  25.5 19.1 %collective-permute-start.3 = (f32[1032,256]{1,0:T(8,128)S(1)}, f32[1032,256]{1,0:T(8,128)}, u32[]{:S(2)}, u32[]{:S(2)}) collective-permute-start(f32[1032,256]{1,0:T(8,128)S(1)} %collective-permute-done.1.refs_2_), channel_id=1, source_target_pairs={{16,17},{17,18},{18,19},{19,16},{20,21},{21,22},{22,23},{23,20},{1... | collective-permute-start | bytes 3170312 | tf_op jit(solution)/shard_map/ppermute | solution.py:245
  44.7 0.0 collective-permute-done.refs_1_
  44.7 1.9 %collective-permute-start.2 = (f32[1032,256]{1,0:T(8,128)S(1)}, f32[1032,256]{1,0:T(8,128)}, u32[]{:S(2)}, u32[]{:S(2)}) collective-permute-start(f32[1032,256]{1,0:T(8,128)S(1)} %collective-permute-done.refs_1_), channel_id=1, source_target_pairs={{4,7},{5,4},{6,5},{7,6},{8,11},{9,8},{10,9},{11,10},{13,12},{14,13}} | collective-permute-start | bytes 3170312 | tf_op jit(solution)/shard_map/ppermute | solution.py:245
  46.6 1.3 %collective-permute-start.6 = (f32[1032,256]{1,0:T(8,128)S(1)}, f32[1032,256]{1,0:T(8,128)}, u32[]{:S(2)}, u32[]{:S(2)}) collective-permute-start(f32[1032,256]{1,0:T(8,128)S(1)} %select_maximum_fusion.refs_0_), channel_id=1, source_target_pairs={{16,4},{25,5},{2,6},{11,7},{24,12},{1,13},{10,14},{19,15},{0,20},{... | collective-permute-start | bytes 3170312 | tf_op jit(solution)/shard_map/ppermute | solution.py:245
  47.9 0.7 dynamic-slice_bitcast_fusion.info_ref
  48.6 6.6 %collective-permute-done.5.refs_2_ = f32[1032,256]{1,0:T(8,128)} collective-permute-done((f32[1032,256]{1,0:T(8,128)S(1)}, f32[1032,256]{1,0:T(8,128)}, u32[]{:S(2)}, u32[]{:S(2)}) %collective-permute-start.5) | collective-permute-done | bytes 1056800 | tf_op jit(solution)/shard_map/ppermute | solution.py:245
  55.2 1.9 %collective-permute-start.8 = (f32[1032,256]{1,0:T(8,128)}, f32[1032,256]{1,0:T(8,128)S(1)}, u32[]{:S(2)}, u32[]{:S(2)}) collective-permute-start(f32[1032,256]{1,0:T(8,128)} %collective-permute-done.5.refs_2_), channel_id=1, source_target_pairs={{4,0},{5,1},{6,2},{0,4},{1,5},{2,6},{12,8},{13,9},{14,10},{8,12},{... | collective-permute-start | bytes 3170312 | tf_op jit(solution)/shard_map/ppermute | solution.py:245
  57.1 0.0 collective-permute-done.4.refs_1_
  57.1 2.4 %collective-permute-start.7 = (f32[1032,256]{1,0:T(8,128)}, f32[1032,256]{1,0:T(8,128)S(1)}, u32[]{:S(2)}, u32[]{:S(2)}) collective-permute-start(f32[1032,256]{1,0:T(8,128)} %collective-permute-done.4.refs_1_), channel_id=1, source_target_pairs={{5,1},{6,2},{7,3},{13,9},{14,10},{15,11},{21,17},{22,18},{23,19},{... | collective-permute-start | bytes 3170312 | tf_op jit(solution)/shard_map/ppermute | solution.py:245
  59.6 7.2 %collective-permute-done.3.refs_4_ = f32[1032,256]{1,0:T(8,128)} collective-permute-done((f32[1032,256]{1,0:T(8,128)S(1)}, f32[1032,256]{1,0:T(8,128)}, u32[]{:S(2)}, u32[]{:S(2)}) %collective-permute-start.3) | collective-permute-done | bytes 1056800 | tf_op jit(solution)/shard_map/ppermute | solution.py:245
  66.8 2.6 %collective-permute-done.2.refs_3_ = f32[1032,256]{1,0:T(8,128)} collective-permute-done((f32[1032,256]{1,0:T(8,128)S(1)}, f32[1032,256]{1,0:T(8,128)}, u32[]{:S(2)}, u32[]{:S(2)}) %collective-permute-start.2) | collective-permute-done | bytes 1056800 | tf_op jit(solution)/shard_map/ppermute | solution.py:245
  69.4 1.3 %shard_map.37.lcode_ref = s32[8,128]{1,0:T(8,128)S(1)} custom-call(s32[10]{0:T(128)S(1)} %dynamic-slice_bitcast_fusion.info_ref, f32[1032,256]{1,0:T(8,128)S(1)} %select_maximum_fusion.refs_0_, f32[1032,256]{1,0:T(8,128)S(1)} %collective-permute-done.refs_1_, f32[1032,256]{1,0:T(8,128)S(1)} %collective-permute-done.1.refs_2_, ...), custom_call_target="tpu_custom_call" | custom-call | flops 99999997952 | bytes 1048576 | tf_op jit(solution)/shard_map/pallas_call | solution.py:269
  70.7 0.0 collective-permute-done.7.refs_4_
  70.7 2.7 %shard_map.38 = (bf16[65,128,256]{2,1,0:T(8,128)(2,1)S(1)}, s32[8,128]{1,0:T(8,128)S(1)}) custom-call(s32[10]{0:T(128)S(1)} %dynamic-slice_bitcast_fusion.info_ref, f32[1032,256]{1,0:T(8,128)S(1)} %select_maximum_fusion.refs_0_, f32[1032,256]{1,0:T(8,128)} %collective-permute-done.4.refs_1_, f32[1032,256]{1,0:T(8,128)} %collective-permute-done.5.refs_2_, ...), custom_call_target="tpu_custom_call" | custom-call | flops 10000000 | bytes 8388608 | tf_op jit(solution)/shard_map/pallas_call | solution.py:256
  73.4 14.5 %shard_map.39 = f32[1024,2048]{1,0:T(8,128)} custom-call(s32[10]{0:T(128)S(1)} %dynamic-slice_bitcast_fusion.info_ref, s32[8,128]{1,0:T(8,128)S(1)} %shard_map.37.lcode_ref, s32[8,128]{1,0:T(8,128)S(1)} %get-tuple-element.7.rcode_ref, bf16[65,128,256]{2,1,0:T(8,128)(2,1)S(1)} %get-tuple-element.8.split_ref, f32[1032,256]{1,0:T(8,128)S(1)} %select_maximum_fusion.refs_0_, ...), custom_call_target="tpu_custom_call" | custom-call | flops 1000000000 | bytes 20971520 | tf_op jit(solution)/shard_map/pallas_call | solution.py:278
  (2 shorter events, 0.0 us)
Async XLA Ops:
  2.2 23.4 %collective-permute-start.1 = (f32[1032,256]{1,0:T(8,128)S(1)}, f32[1032,256]{1,0:T(8,128)S(1)}, u32[]{:S(2)}, u32[]{:S(2)}) collective-permute-start(f32[1032,256]{1,0:T(8,128)S(1)} %select_maximum_fusion.refs_0_), channel_id=1, source_target_pairs={{12,13},{13,14},{14,15},{15,12},{16,17},{17,18},{18,19},{19,16},{2... | collective-permute-start | bytes 3170312 | tf_op jit(solution)/shard_map/ppermute | solution.py:245
  5.4 39.3 %collective-permute-start = (f32[1032,256]{1,0:T(8,128)S(1)}, f32[1032,256]{1,0:T(8,128)S(1)}, u32[]{:S(2)}, u32[]{:S(2)}) collective-permute-start(f32[1032,256]{1,0:T(8,128)S(1)} %select_maximum_fusion.refs_0_), channel_id=1, source_target_pairs={{0,3},{1,0},{2,1},{3,2},{4,7},{5,4},{6,5},{7,6},{8,11},{9,8},{10,9... | collective-permute-start | bytes 3170312 | tf_op jit(solution)/shard_map/ppermute | solution.py:245
  7.5 47.7 %collective-permute-start.5 = (f32[1032,256]{1,0:T(8,128)S(1)}, f32[1032,256]{1,0:T(8,128)}, u32[]{:S(2)}, u32[]{:S(2)}) collective-permute-start(f32[1032,256]{1,0:T(8,128)S(1)} %select_maximum_fusion.refs_0_), channel_id=1, source_target_pairs={{8,0},{17,1},{26,2},{12,4},{21,5},{30,6},{16,8},{25,9},{2,10},{20,... | collective-permute-start | bytes 3170312 | tf_op jit(solution)/shard_map/ppermute | solution.py:245
  8.7 48.4 %collective-permute-start.4 = (f32[1032,256]{1,0:T(8,128)S(1)}, f32[1032,256]{1,0:T(8,128)}, u32[]{:S(2)}, u32[]{:S(2)}) collective-permute-start(f32[1032,256]{1,0:T(8,128)S(1)} %select_maximum_fusion.refs_0_), channel_id=1, source_target_pairs={{9,1},{18,2},{27,3},{13,5},{22,6},{31,7},{17,9},{26,10},{3,11},{21... | collective-permute-start | bytes 3170312 | tf_op jit(solution)/shard_map/ppermute | solution.py:245
  25.5 41.2 %collective-permute-start.3 = (f32[1032,256]{1,0:T(8,128)S(1)}, f32[1032,256]{1,0:T(8,128)}, u32[]{:S(2)}, u32[]{:S(2)}) collective-permute-start(f32[1032,256]{1,0:T(8,128)S(1)} %collective-permute-done.1.refs_2_), channel_id=1, source_target_pairs={{16,17},{17,18},{18,19},{19,16},{20,21},{21,22},{22,23},{23,20},{1... | collective-permute-start | bytes 3170312 | tf_op jit(solution)/shard_map/ppermute | solution.py:245
  44.7 24.7 %collective-permute-start.2 = (f32[1032,256]{1,0:T(8,128)S(1)}, f32[1032,256]{1,0:T(8,128)}, u32[]{:S(2)}, u32[]{:S(2)}) collective-permute-start(f32[1032,256]{1,0:T(8,128)S(1)} %collective-permute-done.refs_1_), channel_id=1, source_target_pairs={{4,7},{5,4},{6,5},{7,6},{8,11},{9,8},{10,9},{11,10},{13,12},{14,13}} | collective-permute-start | bytes 3170312 | tf_op jit(solution)/shard_map/ppermute | solution.py:245
  46.6 24.1 %collective-permute-start.6 = (f32[1032,256]{1,0:T(8,128)S(1)}, f32[1032,256]{1,0:T(8,128)}, u32[]{:S(2)}, u32[]{:S(2)}) collective-permute-start(f32[1032,256]{1,0:T(8,128)S(1)} %select_maximum_fusion.refs_0_), channel_id=1, source_target_pairs={{16,4},{25,5},{2,6},{11,7},{24,12},{1,13},{10,14},{19,15},{0,20},{... | collective-permute-start | bytes 3170312 | tf_op jit(solution)/shard_map/ppermute | solution.py:245
  55.2 15.5 %collective-permute-start.8 = (f32[1032,256]{1,0:T(8,128)}, f32[1032,256]{1,0:T(8,128)S(1)}, u32[]{:S(2)}, u32[]{:S(2)}) collective-permute-start(f32[1032,256]{1,0:T(8,128)} %collective-permute-done.5.refs_2_), channel_id=1, source_target_pairs={{4,0},{5,1},{6,2},{0,4},{1,5},{2,6},{12,8},{13,9},{14,10},{8,12},{... | collective-permute-start | bytes 3170312 | tf_op jit(solution)/shard_map/ppermute | solution.py:245
  57.1 13.6 %collective-permute-start.7 = (f32[1032,256]{1,0:T(8,128)}, f32[1032,256]{1,0:T(8,128)S(1)}, u32[]{:S(2)}, u32[]{:S(2)}) collective-permute-start(f32[1032,256]{1,0:T(8,128)} %collective-permute-done.4.refs_1_), channel_id=1, source_target_pairs={{5,1},{6,2},{7,3},{13,9},{14,10},{15,11},{21,17},{22,18},{23,19},{... | collective-permute-start | bytes 3170312 | tf_op jit(solution)/shard_map/ppermute | solution.py:245
where the time goes:
time: 88 us; the launch traced here: 87.9 us
  starting transfers between devices  35.2 us (40%)
  waiting for transfers between devices  31.3 us (36%)
  Pallas kernels  18.5 us (21%)
  other arithmetic  1.98 us (2%)
    ppermute x9, starting transfers between devices, permute(): lax.ppermute(value, ('row', 'col'), [(s[0] * n_col + s[1], d[0] * n_col +...  35.2 us
    ppermute x9, waiting for transfers between devices, permute(): lax.ppermute(value, ('row', 'col'), [(s[0] * n_col + s[1], d[0] * n_col +...  31.3 us
    pallas_call x1, Pallas kernels, local(): pl.pallas_call(functools.partial(product_kernel, slots, rb, w), out_shape...  14.5 us
    pallas_call x1, Pallas kernels, local(): pl.pallas_call(functools.partial(split_kernel, slots, rb), out_shape=(jax...  2.69 us
  transfers between devices with their start and end apart: 9, of which 4 were waited for; matrix products, arithmetic and copies ran while one was open for 1% of the time, Pallas kernels for 2%

commit v1 on v0

v1 whole, which is shorter than its diff:
```python
import functools

import jax
import jax.numpy as jnp
import numpy as np
from jax import lax
from jax.experimental import pallas as pl
from jax.experimental.pallas import tpu as pltpu
from jax.sharding import PartitionSpec as P

BS = 64
STEPS = 4
UNROLL = 4
EXTRA = 8


def left_offsets(row, ratio, n_col):
    seen = []
    for step in range(STEPS):
        offset = (row + step) // ratio % n_col
        if offset not in seen:
            seen.append(offset)
    return seen


def shift(rows, step, count):
    return [((r, c), (r, (c + step) % count)) for r in rows for c in range(count)]


def left_plan(n_row, n_col, ratio):
    offsets = [left_offsets(row, ratio, n_col) for row in range(n_row)]
    if (n_row, n_col, ratio) != (8, 4, 2):
        perms = []
        for slot in range(max(len(o) for o in offsets)):
            pairs = [
                ((row, (col + offsets[row][slot]) % n_col), (row, col))
                for row in range(n_row)
                for col in range(n_col)
                if slot < len(offsets[row]) and offsets[row][slot] != 0
            ]
            perms.append((0, pairs))
        return perms
    down = shift([r for r in range(8) if 1 in offsets[r] and not {1, 2, 3} <= set(offsets[r])], -1, 4)
    up = shift([r for r in range(8) if 3 in offsets[r] and not {1, 2, 3} <= set(offsets[r])], 1, 4)
    again_down = shift([r for r in range(8) if set(offsets[r]) in ({0, 1, 2}, {1, 2})], -1, 4)
    again_up = shift([r for r in range(8) if set(offsets[r]) in ({2, 3}, {0, 2, 3})], 1, 4)
    down += [((3, c), (3, c - 1)) for c in (1, 2, 3)] + [((3, 0), (6, 3))]
    up += [((3, c), (3, c + 1)) for c in (0, 1, 2)] + [((3, 3), (0, 0))]
    again_down += [((3, 1), (3, 0)), ((3, 2), (3, 1)), ((6, 3), (3, 3))]
    again_up += [((3, 1), (3, 2)), ((3, 2), (3, 3)), ((0, 0), (3, 0))]
    return [(0, down), (0, up), (1, again_down), (2, again_up)]


def right_plan(n_row, n_col, ratio):
    everyone = [(row, col) for row in range(n_row) for col in range(n_col)]
    if (n_row, n_col, ratio) != (8, 4, 2):
        return [
            (0, [(((r + ratio * c + step) % n_row, c), (r, c)) for r, c in everyone if (ratio * c + step) % n_row])
            for step in range(STEPS)
        ]
    first = [(((r + 2 * c) % 8, c), (r, c)) for r, c in everyone if c != 0]
    first += [((r + 1, 0), (r, 0)) for r in range(0, 8, 2)]
    second = [(((r + 2 * c + 2) % 8, c), (r, c)) for r, c in everyone if c != 3]
    second += [((r ^ 1, 3), (r, 3)) for r in range(8)]
    last = [(((r - 1 + 2 * c + 4) % 8, c), (r, c)) for r, c in everyone if r % 2 == 1]
    first_swap = [((r + 1, c), (r, c)) for r, c in everyone if r % 2 == 0 and c != 0]
    second_swap = [((r ^ 1, c), (r, c)) for r, c in everyone if c != 3]
    return [(0, first), (0, second), (0, last), (1, first_swap), (2, second_swap)]


def carry_out(perms, n_row, n_col):
    held = [{(r, c): (r, c) for r in range(n_row) for c in range(n_col)}]
    for source, pairs in perms:
        held.append({dst: held[source][src] for src, dst in pairs})
    return held


def device_table(left_perms, right_perms, n_row, n_col, ratio):
    left_held = carry_out(left_perms, n_row, n_col)
    right_held = carry_out(right_perms, n_row, n_col)
    slots = (ratio - 1 + STEPS - 1) // ratio + 1
    table = np.full((n_row, n_col, 2 * slots + STEPS), -1, np.int32)

    def find(held, device, tile):
        return [i for i, h in enumerate(held) if h.get(device) == tile][0]

    for r in range(n_row):
        for c in range(n_col):
            for slot, offset in enumerate(left_offsets(r, ratio, n_col)):
                tile_col = (c + offset) % n_col
                table[r, c, slot] = find(left_held, (r, c), (r, tile_col))
                table[r, c, slots + STEPS + slot] = (tile_col * ratio - r - ratio * c) % n_row
            for step in range(STEPS):
                table[r, c, slots + step] = find(right_held, (r, c), ((r + ratio * c + step) % n_row, c))
    return table, slots


def fetch(choice, bufs, target, sem):
    for number, buf in enumerate(bufs):
        @pl.when(choice == number)
        def _():
            pltpu.make_async_copy(buf, target, sem).start()


def product_kernel(slots, rb, w, n_right, info_ref, rcode_ref, lcode_ref, *refs):
    out_ref, left, right, acc, value, codes, lsem, rsem, osem = refs[-9:]
    right_bufs, left_bufs = refs[:n_right], refs[:1] + refs[n_right:-9]
    rows, width = left.shape[1] - EXTRA, left.shape[2]
    for step in range(STEPS):
        fetch(info_ref[slots + step], right_bufs, right.at[step], rsem.at[step])
    for slot in range(slots):
        fetch(info_ref[slot], left_bufs, left.at[slot], lsem.at[slot])

    @pl.loop(0, rb)
    def _(r):
        acc[pl.ds(pl.multiple_of(r * BS, BS), BS), :] = jnp.zeros((BS, acc.shape[1]), jnp.float32)

    part_rows = rb // STEPS
    for u in range(UNROLL):
        codes[u] = STEPS << 24
    bounds = [jnp.int32(UNROLL)]
    for part in range(STEPS):
        def listed(i, place):
            for slot in range(slots):
                for k in range(w):
                    code = lcode_ref[slot, (part * part_rows + i) * w + k]
                    codes[place] = code
                    place = place + (code >= 0).astype(jnp.int32)
            return place

        bounds.append(lax.fori_loop(0, part_rows, listed, bounds[-1]))
    for u in range(2 * UNROLL):
        codes[bounds[-1] + u] = STEPS << 24

    for step in range(STEPS):
        pltpu.make_async_copy(right_bufs[0], right.at[step], rsem.at[step]).wait()
    for slot in range(slots):
        @pl.when(info_ref[slot] >= 0)
        def _():
            pltpu.make_async_copy(left_bufs[0], left.at[slot], lsem.at[slot]).wait()

    low = lax.broadcasted_iota(jnp.int32, (BS, 2 * BS), 1) < BS
    half = lax.broadcasted_iota(jnp.int32, (BS, 2 * BS), 1) // BS

    def block_at(index):
        return pl.ds(pl.multiple_of(index * BS, BS), BS)

    def product(code):
        slot = (code >> 8) & 15
        x = left[(code >> 12) & 15, block_at((code >> 16) & 255), pl.ds(pl.multiple_of((slot >> 1) * 2 * BS, 2 * BS), 2 * BS)]
        both = jnp.where(half == (slot & 1), x, pltpu.roll(x, BS, 1))
        hi = both.astype(jnp.bfloat16).astype(jnp.float32)
        lhs = jnp.where(low, hi, both - hi).astype(jnp.bfloat16)
        lhs = jnp.concatenate([lhs, lhs], axis=1)
        y = right[code >> 24, block_at(code & 255), :]
        hi = y.astype(jnp.bfloat16)
        lo = (y - hi.astype(jnp.float32)).astype(jnp.bfloat16)
        rhs = jnp.concatenate([hi, hi, lo, lo], axis=0)
        return jnp.dot(lhs, rhs, preferred_element_type=jnp.float32)

    def add(code, product):
        for pair in range(w // 2):
            x = product[:, pair * 2 * BS : (pair + 1) * 2 * BS]
            turned = pltpu.roll(x, BS, 1)
            for side in range(2):
                place = rcode_ref[code >> 24, (code & 255) * w + 2 * pair + side]
                parity = place >> 16
                picked = jnp.where(parity == side, x, turned)
                picked = jnp.where(half == parity, picked, 0.0)
                base = pl.multiple_of(place & 0xFFFF, 2 * BS)
                acc[block_at((code >> 16) & 255), pl.ds(base, 2 * BS)] += picked

    def out_copy(part):
        at = pl.ds(part * part_rows * BS, part_rows * BS)
        return pltpu.make_async_copy(acc.at[at], out_ref.at[at], osem.at[part])

    groups = [jnp.int32(0)] + [(bound + UNROLL - 1) // UNROLL for bound in bounds[1:]]
    for part in range(STEPS):
        @pl.loop(groups[part], groups[part + 1])
        def _(group):
            for u in range(UNROLL):
                add(codes[group * UNROLL + u], value[u])
            for u in range(UNROLL):
                value[u] = product(codes[(group + 1) * UNROLL + u])

        out_copy(part).start()
    for part in range(STEPS):
        out_copy(part).wait()


def column_codes(left_bufs, right_bufs, info, slots, n_row, ratio, rows, rb, w):
    def chosen(bufs, choice):
        cols = jnp.stack([buf[rows, : rb * w] for buf in bufs]).astype(jnp.int32)
        return jnp.sum(jnp.where(choice[:, None, None] == jnp.arange(len(bufs))[None, :, None], cols, 0), axis=1)

    cols = chosen(left_bufs, info[:slots])
    place = jnp.arange(rb * w, dtype=jnp.int32)[None, :]
    slot = jnp.arange(slots, dtype=jnp.int32)[:, None]
    step = (info[slots + STEPS :][:, None] + cols // rb) % n_row
    code = cols % rb | place % w << 8 | slot << 12 | place // w << 16 | step << 24
    valid = (cols >= 0) & (step < STEPS) & (info[:slots] >= 0)[:, None]
    left_code = jnp.where(valid, code, -1)
    cols = chosen(right_bufs, info[slots : slots + STEPS])
    cols = jnp.concatenate([cols, jnp.full((1, rb * w), -1, jnp.int32)])
    right_code = jnp.where(cols < 0, 2 << 16, (cols >> 1) * 2 * BS | (cols & 1) << 16)
    return left_code, right_code


def local(p_cols, p_data):
    n_row, n_col = lax.axis_size("row"), lax.axis_size("col")
    ratio = n_row // n_col
    row_id, col_id = lax.axis_index("row"), lax.axis_index("col")
    rb, w = p_cols.shape
    rows, width = p_data.shape
    left_perms = left_plan(n_row, n_col, ratio)
    right_perms = right_plan(n_row, n_col, ratio)
    table, slots = device_table(left_perms, right_perms, n_row, n_col, ratio)
    info = jnp.asarray(table)[row_id, col_id]

    cols = jnp.pad(p_cols.astype(jnp.float32).reshape(1, -1), ((0, EXTRA - 1), (0, width - rb * w)))
    own = jnp.concatenate([p_data, cols], axis=0)

    def permute(value, pairs):
        return lax.ppermute(value, ("row", "col"), [(s[0] * n_col + s[1], d[0] * n_col + d[1]) for s, d in pairs])

    left_bufs, right_bufs = [own], [own]
    for source, pairs in right_perms:
        right_bufs.append(permute(right_bufs[source], pairs))
    for source, pairs in left_perms:
        left_bufs.append(permute(left_bufs[source], pairs))
    left_code, right_code = column_codes(left_bufs, right_bufs, info, slots, n_row, ratio, rows, rb, w)

    out_shape = jax.ShapeDtypeStruct((rows, rb * ratio * BS), jnp.float32)
    smem = pl.BlockSpec(memory_space=pltpu.SMEM)
    hbm = pl.BlockSpec(memory_space=pl.ANY)
    dma = pltpu.SemaphoreType.DMA
    bufs = right_bufs + left_bufs[1:]
    return pl.pallas_call(
        functools.partial(product_kernel, slots, rb, w, len(right_bufs)),
        out_shape=out_shape,
        in_specs=[smem, smem, smem] + [hbm] * len(bufs),
        out_specs=hbm,
        scratch_shapes=[
            pltpu.VMEM((slots, rows + EXTRA, width), jnp.float32),
            pltpu.VMEM((STEPS + 1, rows + EXTRA, width), jnp.float32),
            pltpu.VMEM(out_shape.shape, jnp.float32),
            pltpu.VMEM((UNROLL, BS, width), jnp.float32),
            pltpu.SMEM((slots * rb * w + 4 * UNROLL,), jnp.int32),
            dma((slots,)),
            dma((STEPS,)),
            dma((STEPS,)),
        ],
        compiler_params=pltpu.CompilerParams(vmem_limit_bytes=24 << 20),
        cost_estimate=pl.CostEstimate(flops=10**9, bytes_accessed=20 << 20, transcendentals=0),
    )(info, right_code, left_code, *bufs)


def solution(mesh):
    in_specs = (P("row", "col"), P("row", "col"))
    return jax.shard_map(local, mesh=mesh, in_specs=in_specs, out_specs=P("row", "col"), check_vma=False)
```

time: 88 us -> 85.6 us (0.973)
  the two profiles are of different devices: /device:TPU:11 before, /device:TPU:2 now
where the time goes in v1:
time: 85.6 us; the launch traced here: 84.7 us
  waiting for transfers between devices  43.1 us (50%)
  starting transfers between devices  19.6 us (23%)
  Pallas kernels  10.1 us (12%)
  local copies, waits for them, and re-layouts  9.57 us (11%)
  other arithmetic  2.29 us (3%)
    ppermute x9, waiting for transfers between devices, permute(): lax.ppermute(value, ('row', 'col'), [(s[0] * n_col + s[1], d[0] * n_col +...  43.1 us
    ppermute x9, starting transfers between devices, permute(): lax.ppermute(value, ('row', 'col'), [(s[0] * n_col + s[1], d[0] * n_col +...  19.6 us
    pallas_call x1, Pallas kernels, local(): pl.pallas_call(functools.partial(product_kernel, slots, rb, w, len(right_...  10.1 us
    unnamed x8, local copies, waits for them, and re-layouts  4.44 us
    slice x9, local copies, waits for them, and re-layouts, chosen(): cols = jnp.stack([buf[rows, :rb * w] for buf in bufs]).astype(jnp.int32)  3.4 us
  transfers between devices with their start and end apart: 9, of which 2 were waited for; matrix products, arithmetic and copies ran while one was open for 5% of the time, Pallas kernels for 0%

profile of v1, /device:TPU:2, one launch (start us, length us, event | category | flops | bytes accessed | tf_op | source)
XLA Modules:
  0.0 84.7 jit_solution(4281632022323439676)
XLA Ops:
  0.0 0.7 convert_element_type.11
  0.9 1.3 %select_maximum_fusion.refs_0_ = f32[1032,256]{1,0:T(8,128)S(1)} fusion(f32[1,64]{1,0:T(1,128)S(1)} %reshape.132, f32[1024,256]{1,0:T(8,128)} %param.4), kind=kLoop, calls=%fused_computation | loop fusion | flops 792576 | bytes 2105600 | tf_op jit(solution)/shard_map/concatenate | solution.py:221
  2.2 0.7 collective-permute-start.6
  2.9 5.5 %collective-permute-start.5 = (f32[1032,256]{1,0:T(8,128)S(1)}, f32[1032,256]{1,0:T(8,128)S(1)}, u32[]{:S(2)}, u32[]{:S(2)}) collective-permute-start(f32[1032,256]{1,0:T(8,128)S(1)} %select_maximum_fusion.refs_0_), channel_id=1, source_target_pairs={{0,3},{1,0},{2,1},{3,2},{4,7},{5,4},{6,5},{7,6},{8,11},{9,8},{10,9... | collective-permute-start | bytes 3170312 | tf_op jit(solution)/shard_map/ppermute | solution.py:224
  9.0 1.3 %collective-permute-start = (f32[1032,256]{1,0:T(8,128)S(1)}, f32[1032,256]{1,0:T(8,128)}, u32[]{:S(2)}, u32[]{:S(2)}) collective-permute-start(f32[1032,256]{1,0:T(8,128)S(1)} %select_maximum_fusion.refs_0_), channel_id=1, source_target_pairs={{9,1},{18,2},{27,3},{13,5},{22,6},{31,7},{17,9},{26,10},{3,11},{21... | collective-permute-start | bytes 3170312 | tf_op jit(solution)/shard_map/ppermute | solution.py:224
  10.3 5.2 %collective-permute-start.2 = (f32[1032,256]{1,0:T(8,128)S(1)}, f32[1032,256]{1,0:T(8,128)}, u32[]{:S(2)}, u32[]{:S(2)}) collective-permute-start(f32[1032,256]{1,0:T(8,128)S(1)} %select_maximum_fusion.refs_0_), channel_id=1, source_target_pairs={{16,4},{25,5},{2,6},{11,7},{24,12},{1,13},{10,14},{19,15},{0,20},{... | collective-permute-start | bytes 3170312 | tf_op jit(solution)/shard_map/ppermute | solution.py:224
  15.5 0.7 constant_dynamic-slice_fusion
  16.2 0.7 fusion.14.info_ref
  16.9 0.7 collective-permute-start.8
  17.6 24.6 %collective-permute-done.5.refs_6_ = f32[1032,256]{1,0:T(8,128)S(1)} collective-permute-done((f32[1032,256]{1,0:T(8,128)S(1)}, f32[1032,256]{1,0:T(8,128)S(1)}, u32[]{:S(2)}, u32[]{:S(2)}) %collective-permute-start.5) | collective-permute-done | bytes 1056800 | tf_op jit(solution)/shard_map/ppermute | solution.py:224
  42.2 1.9 %collective-permute-start.7 = (f32[1032,256]{1,0:T(8,128)S(1)}, f32[1032,256]{1,0:T(8,128)S(1)}, u32[]{:S(2)}, u32[]{:S(2)}) collective-permute-start(f32[1032,256]{1,0:T(8,128)S(1)} %collective-permute-done.5.refs_6_), channel_id=1, source_target_pairs={{4,7},{5,4},{6,5},{7,6},{8,11},{9,8},{10,9},{11,10},{13,12},{14,13... | collective-permute-start | bytes 3170312 | tf_op jit(solution)/shard_map/ppermute | solution.py:224
  44.1 1.9 %collective-permute-start.4 = (f32[1032,256]{1,0:T(8,128)}, f32[1032,256]{1,0:T(8,128)}, u32[]{:S(2)}, u32[]{:S(2)}) collective-permute-start(f32[1032,256]{1,0:T(8,128)} %collective-permute-done.1.refs_2_), channel_id=1, source_target_pairs={{4,0},{5,1},{6,2},{0,4},{1,5},{2,6},{12,8},{13,9},{14,10},{8,12},{... | collective-permute-start | bytes 3170312 | tf_op jit(solution)/shard_map/ppermute | solution.py:224
  46.1 1.7 %collective-permute-start.3 = (f32[1032,256]{1,0:T(8,128)}, f32[1032,256]{1,0:T(8,128)}, u32[]{:S(2)}, u32[]{:S(2)}) collective-permute-start(f32[1032,256]{1,0:T(8,128)} %collective-permute-done.refs_1_), channel_id=1, source_target_pairs={{5,1},{6,2},{7,3},{13,9},{14,10},{15,11},{21,17},{22,18},{23,19},{... | collective-permute-start | bytes 3170312 | tf_op jit(solution)/shard_map/ppermute | solution.py:224
  47.9 0.7 slice.55
  48.6 0.7 slice.54
  49.3 0.7 slice.56
  50.0 1.0 %copy-done = f32[1032,256]{1,0:T(8,128)} copy-done((f32[1032,256]{1,0:T(8,128)}, f32[1032,256]{1,0:T(8,128)S(1)}, u32[]{:S(2)}) %copy-start) | copy-done | bytes 1056792
  51.0 18.5 %collective-permute-done.7.refs_8_ = f32[1032,256]{1,0:T(8,128)S(1)} collective-permute-done((f32[1032,256]{1,0:T(8,128)S(1)}, f32[1032,256]{1,0:T(8,128)S(1)}, u32[]{:S(2)}, u32[]{:S(2)}) %collective-permute-start.7) | collective-permute-done | bytes 1056800 | tf_op jit(solution)/shard_map/ppermute | solution.py:224
  69.5 1.0 %copy-done.2 = f32[1032,256]{1,0:T(8,128)} copy-done((f32[1032,256]{1,0:T(8,128)}, f32[1032,256]{1,0:T(8,128)S(1)}, u32[]{:S(2)}) %copy-start.2) | copy-done | bytes 1056792
  70.5 0.7 slice.58
  71.2 0.7 slice.57
  72.1 1.2 %copy-done.1 = f32[1032,256]{1,0:T(8,128)S(1)} copy-done((f32[1032,256]{1,0:T(8,128)S(1)}, f32[1032,256]{1,0:T(8,128)}, u32[]{:S(2)}) %copy-start.1) | copy-done | bytes 1056792
  73.4 1.2 %copy-done.3 = f32[1032,256]{1,0:T(8,128)S(1)} copy-done((f32[1032,256]{1,0:T(8,128)S(1)}, f32[1032,256]{1,0:T(8,128)}, u32[]{:S(2)}) %copy-start.3) | copy-done | bytes 1056792
  74.6 10.1 %shard_map.37 = f32[1024,2048]{1,0:T(8,128)} custom-call(s32[10]{0:T(128)S(1)} %fusion.14.info_ref, s32[5,64]{1,0:T(8,128)S(1)} %fusion.2.rcode_ref, s32[3,64]{1,0:T(4,128)S(1)} %fusion.10.lcode_ref, f32[1032,256]{1,0:T(8,128)S(1)} %select_maximum_fusion.refs_0_, f32[1032,256]{1,0:T(8,128)} %collective-permute-done.refs_1_, ...), custom_call_target="tpu_custom_call" | custom-call | flops 1000000000 | bytes 20971520 | tf_op jit(solution)/shard_map/pallas_call | solution.py:238
  (33 shorter events, 1.3 us)
Async XLA Ops:
  2.2 14.7 %collective-permute-start.6 = (f32[1032,256]{1,0:T(8,128)S(1)}, f32[1032,256]{1,0:T(8,128)S(1)}, u32[]{:S(2)}, u32[]{:S(2)}) collective-permute-start(f32[1032,256]{1,0:T(8,128)S(1)} %select_maximum_fusion.refs_0_), channel_id=1, source_target_pairs={{16,17},{17,18},{18,19},{19,16},{20,21},{21,22},{22,23},{23,20},{2... | collective-permute-start | bytes 3170312 | tf_op jit(solution)/shard_map/ppermute | solution.py:224
  2.9 39.3 %collective-permute-start.5 = (f32[1032,256]{1,0:T(8,128)S(1)}, f32[1032,256]{1,0:T(8,128)S(1)}, u32[]{:S(2)}, u32[]{:S(2)}) collective-permute-start(f32[1032,256]{1,0:T(8,128)S(1)} %select_maximum_fusion.refs_0_), channel_id=1, source_target_pairs={{0,3},{1,0},{2,1},{3,2},{4,7},{5,4},{6,5},{7,6},{8,11},{9,8},{10,9... | collective-permute-start | bytes 3170312 | tf_op jit(solution)/shard_map/ppermute | solution.py:224
  8.4 35.7 %collective-permute-start.1 = (f32[1032,256]{1,0:T(8,128)S(1)}, f32[1032,256]{1,0:T(8,128)}, u32[]{:S(2)}, u32[]{:S(2)}) collective-permute-start(f32[1032,256]{1,0:T(8,128)S(1)} %select_maximum_fusion.refs_0_), channel_id=1, source_target_pairs={{8,0},{17,1},{26,2},{12,4},{21,5},{30,6},{16,8},{25,9},{2,10},{20,... | collective-permute-start | bytes 3170312 | tf_op jit(solution)/shard_map/ppermute | solution.py:224
  9.0 37.1 %collective-permute-start = (f32[1032,256]{1,0:T(8,128)S(1)}, f32[1032,256]{1,0:T(8,128)}, u32[]{:S(2)}, u32[]{:S(2)}) collective-permute-start(f32[1032,256]{1,0:T(8,128)S(1)} %select_maximum_fusion.refs_0_), channel_id=1, source_target_pairs={{9,1},{18,2},{27,3},{13,5},{22,6},{31,7},{17,9},{26,10},{3,11},{21... | collective-permute-start | bytes 3170312 | tf_op jit(solution)/shard_map/ppermute | solution.py:224
  10.3 39.0 %collective-permute-start.2 = (f32[1032,256]{1,0:T(8,128)S(1)}, f32[1032,256]{1,0:T(8,128)}, u32[]{:S(2)}, u32[]{:S(2)}) collective-permute-start(f32[1032,256]{1,0:T(8,128)S(1)} %select_maximum_fusion.refs_0_), channel_id=1, source_target_pairs={{16,4},{25,5},{2,6},{11,7},{24,12},{1,13},{10,14},{19,15},{0,20},{... | collective-permute-start | bytes 3170312 | tf_op jit(solution)/shard_map/ppermute | solution.py:224
  16.9 33.1 %collective-permute-start.8 = (f32[1032,256]{1,0:T(8,128)S(1)}, f32[1032,256]{1,0:T(8,128)S(1)}, u32[]{:S(2)}, u32[]{:S(2)}) collective-permute-start(f32[1032,256]{1,0:T(8,128)S(1)} %collective-permute-done.6.refs_7_), channel_id=1, source_target_pairs={{16,17},{17,18},{18,19},{19,16},{20,21},{21,22},{22,23},{23,20},{1... | collective-permute-start | bytes 3170312 | tf_op jit(solution)/shard_map/ppermute | solution.py:224
  42.2 27.2 %collective-permute-start.7 = (f32[1032,256]{1,0:T(8,128)S(1)}, f32[1032,256]{1,0:T(8,128)S(1)}, u32[]{:S(2)}, u32[]{:S(2)}) collective-permute-start(f32[1032,256]{1,0:T(8,128)S(1)} %collective-permute-done.5.refs_6_), channel_id=1, source_target_pairs={{4,7},{5,4},{6,5},{7,6},{8,11},{9,8},{10,9},{11,10},{13,12},{14,13... | collective-permute-start | bytes 3170312 | tf_op jit(solution)/shard_map/ppermute | solution.py:224
  44.1 26.3 %collective-permute-start.4 = (f32[1032,256]{1,0:T(8,128)}, f32[1032,256]{1,0:T(8,128)}, u32[]{:S(2)}, u32[]{:S(2)}) collective-permute-start(f32[1032,256]{1,0:T(8,128)} %collective-permute-done.1.refs_2_), channel_id=1, source_target_pairs={{4,0},{5,1},{6,2},{0,4},{1,5},{2,6},{12,8},{13,9},{14,10},{8,12},{... | collective-permute-start | bytes 3170312 | tf_op jit(solution)/shard_map/ppermute | solution.py:224
  46.1 25.1 %collective-permute-start.3 = (f32[1032,256]{1,0:T(8,128)}, f32[1032,256]{1,0:T(8,128)}, u32[]{:S(2)}, u32[]{:S(2)}) collective-permute-start(f32[1032,256]{1,0:T(8,128)} %collective-permute-done.refs_1_), channel_id=1, source_target_pairs={{5,1},{6,2},{7,3},{13,9},{14,10},{15,11},{21,17},{22,18},{23,19},{... | collective-permute-start | bytes 3170312 | tf_op jit(solution)/shard_map/ppermute | solution.py:224
  50.0 1.0 %copy-start = (f32[1032,256]{1,0:T(8,128)}, f32[1032,256]{1,0:T(8,128)S(1)}, u32[]{:S(2)}) copy-start(f32[1032,256]{1,0:T(8,128)S(1)} %collective-permute-done.8.refs_9_) | copy-start | bytes 3170308
  69.5 1.0 %copy-start.2 = (f32[1032,256]{1,0:T(8,128)}, f32[1032,256]{1,0:T(8,128)S(1)}, u32[]{:S(2)}) copy-start(f32[1032,256]{1,0:T(8,128)S(1)} %collective-permute-done.7.refs_8_) | copy-start | bytes 3170308
  72.1 1.2 %copy-start.1 = (f32[1032,256]{1,0:T(8,128)S(1)}, f32[1032,256]{1,0:T(8,128)}, u32[]{:S(2)}) copy-start(f32[1032,256]{1,0:T(8,128)} %copy-done) | copy-start | bytes 3170308
  73.4 1.2 %copy-start.3 = (f32[1032,256]{1,0:T(8,128)S(1)}, f32[1032,256]{1,0:T(8,128)}, u32[]{:S(2)}) copy-start(f32[1032,256]{1,0:T(8,128)} %copy-done.2) | copy-start | bytes 3170308

commit v2 on v1

--- a/solution.py
+++ b/solution.py
@@ -44,10 +44,10 @@
     up = shift([r for r in range(8) if 3 in offsets[r] and not {1, 2, 3} <= set(offsets[r])], 1, 4)
     again_down = shift([r for r in range(8) if set(offsets[r]) in ({0, 1, 2}, {1, 2})], -1, 4)
     again_up = shift([r for r in range(8) if set(offsets[r]) in ({2, 3}, {0, 2, 3})], 1, 4)
-    down += [((3, c), (3, c - 1)) for c in (1, 2, 3)] + [((3, 0), (6, 3))]
-    up += [((3, c), (3, c + 1)) for c in (0, 1, 2)] + [((3, 3), (0, 0))]
-    again_down += [((3, 1), (3, 0)), ((3, 2), (3, 1)), ((6, 3), (3, 3))]
-    again_up += [((3, 1), (3, 2)), ((3, 2), (3, 3)), ((0, 0), (3, 0))]
+    down += [((3, c), (3, c - 1)) for c in (1, 2, 3)] + [((3, 0), (6, 0))]
+    up += [((3, c), (3, c + 1)) for c in (0, 1, 2)] + [((3, 3), (0, 3))]
+    again_down += [((3, 1), (3, 0)), ((3, 2), (3, 1)), ((6, 0), (3, 3))]
+    again_up += [((3, 1), (3, 2)), ((3, 2), (3, 3)), ((0, 3), (3, 0))]
     return [(0, down), (0, up), (1, again_down), (2, again_up)]
 
 
@@ -58,20 +58,27 @@
             (0, [(((r + ratio * c + step) % n_row, c), (r, c)) for r, c in everyone if (ratio * c + step) % n_row])
             for step in range(STEPS)
         ]
-    first = [(((r + 2 * c) % 8, c), (r, c)) for r, c in everyone if c != 0]
-    first += [((r + 1, 0), (r, 0)) for r in range(0, 8, 2)]
-    second = [(((r + 2 * c + 2) % 8, c), (r, c)) for r, c in everyone if c != 3]
-    second += [((r ^ 1, 3), (r, 3)) for r in range(8)]
-    last = [(((r - 1 + 2 * c + 4) % 8, c), (r, c)) for r, c in everyone if r % 2 == 1]
-    first_swap = [((r + 1, c), (r, c)) for r, c in everyone if r % 2 == 0 and c != 0]
-    second_swap = [((r ^ 1, c), (r, c)) for r, c in everyone if c != 3]
-    return [(0, first), (0, second), (0, last), (1, first_swap), (2, second_swap)]
+    along_y = [((r ^ 4, c), (r, c)) for r, c in everyone]
+    along_x = [((r ^ 2, c), (r, c)) for r, c in everyone]
+    even = [((r ^ 2, c), (r, c)) for r, c in everyone if r % 2 == 0]
+    odd = [((r ^ 4, c), (r, c)) for r, c in everyone if r % 2 == 1]
+    perms = [(0, along_y), (0, along_x), (1, even), (2, odd)]
+    held = carry_out(perms, n_row, n_col)
+    swap = [((r ^ 1, c), (r, c)) for r, c in everyone]
+    for buffers in ((0, 1), (2, 3, 4)):
+        choice = {}
+        for r, c in everyone:
+            needs = [((r ^ 1) + 2 * c + step) % 8 for step in range(STEPS)]
+            choice[r, c] = [b for b in buffers if held[b].get((r, c)) in [(k, c) for k in needs]][0]
+        perms.append((choice, swap))
+    return perms
 
 
 def carry_out(perms, n_row, n_col):
     held = [{(r, c): (r, c) for r in range(n_row) for c in range(n_col)}]
     for source, pairs in perms:
-        held.append({dst: held[source][src] for src, dst in pairs})
+        pick = source.get if isinstance(source, dict) else lambda device: source
+        held.append({dst: held[pick(src)][src] for src, dst in pairs})
     return held
 
 
@@ -102,18 +109,57 @@
             pltpu.make_async_copy(buf, target, sem).start()
 
 
-def product_kernel(slots, rb, w, n_right, info_ref, rcode_ref, lcode_ref, *refs):
-    out_ref, left, right, acc, value, codes, lsem, rsem, osem = refs[-9:]
-    right_bufs, left_bufs = refs[:n_right], refs[:1] + refs[n_right:-9]
+def product_kernel(slots, n_row, ratio, rb, w, n_right, info_ref, *refs):
+    out_ref, left, right, acc, value, cols, coded, scalars, codes, lsem, rsem, osem, csem = refs[-13:]
+    right_bufs, left_bufs = refs[:n_right], refs[:1] + refs[n_right:-13]
     rows, width = left.shape[1] - EXTRA, left.shape[2]
+    names = pl.ds(rows, EXTRA)
+    for slot in range(slots):
+        fetch(info_ref[slot], [buf.at[names] for buf in left_bufs], cols.at[slot], csem.at[slot])
+    for step in range(STEPS):
+        choice = info_ref[slots + step]
+        fetch(choice, [buf.at[names] for buf in right_bufs], cols.at[slots + step], csem.at[slots + step])
     for step in range(STEPS):
         fetch(info_ref[slots + step], right_bufs, right.at[step], rsem.at[step])
     for slot in range(slots):
         fetch(info_ref[slot], left_bufs, left.at[slot], lsem.at[slot])
 
-    @pl.loop(0, rb)
-    def _(r):
-        acc[pl.ds(pl.multiple_of(r * BS, BS), BS), :] = jnp.zeros((BS, acc.shape[1]), jnp.float32)
+    def clear(first, last):
+        @pl.loop(first, last)
+        def _(r):
+            acc[pl.ds(pl.multiple_of(r * BS, BS), BS), :] = jnp.zeros((BS, acc.shape[1]), jnp.float32)
+
+    clear(0, rb // 4)
+    lanes = scalars.shape[1]
+    place = lax.broadcasted_iota(jnp.int32, (1, lanes), 1)
+    for slot in range(slots):
+        used = info_ref[slot] >= 0
+
+        @pl.when(used)
+        def _():
+            pltpu.make_async_copy(left_bufs[0].at[names], cols.at[slot], csem.at[slot]).wait()
+
+        inner = cols[slot, 0:1, 0:lanes].astype(jnp.int32)
+        valid = (inner >= 0) & (place < rb * w)
+        step = jnp.full(inner.shape, info_ref[slots + STEPS + slot], jnp.int32)
+        for _ in range(ratio - 1):
+            beyond = inner >= rb
+            step = jnp.where(beyond, step + 1, step)
+            inner = jnp.where(beyond, inner - rb, inner)
+        step = jnp.where(step >= n_row, step - n_row, step)
+        code = inner | (place & (w - 1)) << 8 | slot << 12 | (place // w) << 16 | step << 24
+        valid = valid & (step < STEPS)
+        coded[slot : slot + 1, :] = jnp.where(valid, jnp.where(used, code, -1), -1)
+    for step in range(STEPS):
+        pltpu.make_async_copy(right_bufs[0].at[names], cols.at[slots + step], csem.at[slots + step]).wait()
+        col = cols[slots + step, 0:1, 0:lanes].astype(jnp.int32)
+        code = (col >> 1) * 2 * BS | (col & 1) << 16
+        coded[slots + step : slots + step + 1, :] = jnp.where(col < 0, 2 << 16, code)
+    coded[slots + STEPS : slots + STEPS + 1, :] = jnp.full((1, lanes), 2 << 16, jnp.int32)
+    to_scalars = pltpu.make_async_copy(coded, scalars, csem.at[slots + STEPS])
+    to_scalars.start()
+    clear(rb // 4, rb)
+    to_scalars.wait()
 
     part_rows = rb // STEPS
     for u in range(UNROLL):
@@ -123,7 +169,7 @@
         def listed(i, place):
             for slot in range(slots):
                 for k in range(w):
-                    code = lcode_ref[slot, (part * part_rows + i) * w + k]
+                    code = scalars[slot, (part * part_rows + i) * w + k]
                     codes[place] = code
                     place = place + (code >= 0).astype(jnp.int32)
             return place
@@ -163,7 +209,7 @@
             x = product[:, pair * 2 * BS : (pair + 1) * 2 * BS]
             turned = pltpu.roll(x, BS, 1)
             for side in range(2):
-                place = rcode_ref[code >> 24, (code & 255) * w + 2 * pair + side]
+                place = scalars[slots + (code >> 24), (code & 255) * w + 2 * pair + side]
                 parity = place >> 16
                 picked = jnp.where(parity == side, x, turned)
                 picked = jnp.where(half == parity, picked, 0.0)
@@ -186,24 +232,6 @@
         out_copy(part).start()
     for part in range(STEPS):
         out_copy(part).wait()
-
-
-def column_codes(left_bufs, right_bufs, info, slots, n_row, ratio, rows, rb, w):
-    def chosen(bufs, choice):
-        cols = jnp.stack([buf[rows, : rb * w] for buf in bufs]).astype(jnp.int32)
-        return jnp.sum(jnp.where(choice[:, None, None] == jnp.arange(len(bufs))[None, :, None], cols, 0), axis=1)
-
-    cols = chosen(left_bufs, info[:slots])
-    place = jnp.arange(rb * w, dtype=jnp.int32)[None, :]
-    slot = jnp.arange(slots, dtype=jnp.int32)[:, None]
-    step = (info[slots + STEPS :][:, None] + cols // rb) % n_row
-    code = cols % rb | place % w << 8 | slot << 12 | place // w << 16 | step << 24
-    valid = (cols >= 0) & (step < STEPS) & (info[:slots] >= 0)[:, None]
-    left_code = jnp.where(valid, code, -1)
-    cols = chosen(right_bufs, info[slots : slots + STEPS])
-    cols = jnp.concatenate([cols, jnp.full((1, rb * w), -1, jnp.int32)])
-    right_code = jnp.where(cols < 0, 2 << 16, (cols >> 1) * 2 * BS | (cols & 1) << 16)
-    return left_code, right_code
 
 
 def local(p_cols, p_data):
@@ -223,36 +251,49 @@
     def permute(value, pairs):
         return lax.ppermute(value, ("row", "col"), [(s[0] * n_col + s[1], d[0] * n_col + d[1]) for s, d in pairs])
 
-    left_bufs, right_bufs = [own], [own]
-    for source, pairs in right_perms:
-        right_bufs.append(permute(right_bufs[source], pairs))
-    for source, pairs in left_perms:
-        left_bufs.append(permute(left_bufs[source], pairs))
-    left_code, right_code = column_codes(left_bufs, right_bufs, info, slots, n_row, ratio, rows, rb, w)
-
+    def carry(perms):
+        bufs = [own]
+        for source, pairs in perms:
+            if isinstance(source, dict):
+                picks = np.array([[source[r, c] for c in range(n_col)] for r in range(n_row)], np.int32)
+                pick = jnp.asarray(picks)[row_id, col_id]
+                first, *others = sorted(set(source.values()))
+                value = bufs[first]
+                for other in others:
+                    value = jnp.where(pick == other, bufs[other], value)
+            else:
+                value = bufs[source]
+            bufs.append(lax.ppermute(value, ("row", "col"), [(s[0] * n_col + s[1], d[0] * n_col + d[1]) for s, d in pairs]))
+        return bufs
+
+    right_bufs, left_bufs = carry(right_perms), carry(left_perms)
     out_shape = jax.ShapeDtypeStruct((rows, rb * ratio * BS), jnp.float32)
     smem = pl.BlockSpec(memory_space=pltpu.SMEM)
     hbm = pl.BlockSpec(memory_space=pl.ANY)
     dma = pltpu.SemaphoreType.DMA
     bufs = right_bufs + left_bufs[1:]
     return pl.pallas_call(
-        functools.partial(product_kernel, slots, rb, w, len(right_bufs)),
+        functools.partial(product_kernel, slots, n_row, ratio, rb, w, len(right_bufs)),
         out_shape=out_shape,
-        in_specs=[smem, smem, smem] + [hbm] * len(bufs),
+        in_specs=[smem] + [hbm] * len(bufs),
         out_specs=hbm,
         scratch_shapes=[
             pltpu.VMEM((slots, rows + EXTRA, width), jnp.float32),
             pltpu.VMEM((STEPS + 1, rows + EXTRA, width), jnp.float32),
             pltpu.VMEM(out_shape.shape, jnp.float32),
             pltpu.VMEM((UNROLL, BS, width), jnp.float32),
+            pltpu.VMEM((slots + STEPS, EXTRA, width), jnp.float32),
+            pltpu.VMEM((16, 128), jnp.int32),
+            pltpu.SMEM((16, 128), jnp.int32),
             pltpu.SMEM((slots * rb * w + 4 * UNROLL,), jnp.int32),
             dma((slots,)),
             dma((STEPS,)),
             dma((STEPS,)),
+            dma((slots + STEPS + 1,)),
         ],
         compiler_params=pltpu.CompilerParams(vmem_limit_bytes=24 << 20),
         cost_estimate=pl.CostEstimate(flops=10**9, bytes_accessed=20 << 20, transcendentals=0),
-    )(info, right_code, left_code, *bufs)
+    )(info, *bufs)
 
 
 def solution(mesh):

time: 85.6 us -> 80.1 us (0.936)
  the two profiles are of different devices: /device:TPU:2 before, /device:TPU:3 now
where the time goes in v2:
time: 80.1 us; the launch traced here: 79.2 us
  waiting for transfers between devices  42.3 us (53%)
  starting transfers between devices  16.3 us (20%)
  Pallas kernels  10.3 us (13%)
  other arithmetic  4.84 us (6%)
  local copies, waits for them, and re-layouts  3.41 us (4%)
  between operations  2.04 us (3%)
    ppermute x10, waiting for transfers between devices, carry(): lax.ppermute(value, ('row', 'col'), [(s[0] * n_col + s[1], d[0] * n_col +...  42.3 us
    ppermute x10, starting transfers between devices, carry(): lax.ppermute(value, ('row', 'col'), [(s[0] * n_col + s[1], d[0] * n_col +...  16.3 us
    pallas_call x1, Pallas kernels, local(): pl.pallas_call(functools.partial(product_kernel, slots, n_row, ratio, rb,...  10.3 us
    select_n x2, other arithmetic, carry(): value = jnp.where(pick == other, bufs[other], value)  2.86 us
    dynamic_slice x2, local copies, waits for them, and re-layouts, carry(): pick = jnp.asarray(picks)[row_id, col_id]  2.55 us
  transfers between devices with their start and end apart: 10, of which 3 were waited for; matrix products, arithmetic and copies ran while one was open for 8% of the time, Pallas kernels for 0%

profile of v2, /device:TPU:3, one launch (start us, length us, event | category | flops | bytes accessed | tf_op | source)
XLA Modules:
  0.0 79.2 jit_solution(9100989263663711601)
XLA Ops:
  0.0 0.7 convert_element_type.5
  0.7 0.1 copy.7
  0.8 0.1 reshape.9
  0.9 1.3 %select_maximum_fusion.refs_0_ = f32[1032,256]{1,0:T(8,128)S(1)} fusion(f32[1,64]{1,0:T(1,128)S(1)} %reshape.9, f32[1024,256]{1,0:T(8,128)} %param.6), kind=kLoop, calls=%fused_computation | loop fusion | flops 792576 | bytes 2105600 | tf_op jit(solution)/shard_map/concatenate | solution.py:249
  2.2 0.1 collective-permute-start.1
  2.2 1.5 %collective-permute-start = (f32[1032,256]{1,0:T(8,128)S(1)}, f32[1032,256]{1,0:T(8,128)S(1)}, u32[]{:S(2)}, u32[]{:S(2)}) collective-permute-start(f32[1032,256]{1,0:T(8,128)S(1)} %select_maximum_fusion.refs_0_), channel_id=1, source_target_pairs={{16,0},{17,1},{18,2},{19,3},{20,4},{21,5},{22,6},{23,7},{24,8},{25... | collective-permute-start | bytes 3170312 | tf_op jit(solution)/shard_map/ppermute | solution.py:266
  3.7 4.2 %collective-permute-start.7 = (f32[1032,256]{1,0:T(8,128)S(1)}, f32[1032,256]{1,0:T(8,128)}, u32[]{:S(2)}, u32[]{:S(2)}) collective-permute-start(f32[1032,256]{1,0:T(8,128)S(1)} %select_maximum_fusion.refs_0_), channel_id=1, source_target_pairs={{16,17},{17,18},{18,19},{19,16},{20,21},{21,22},{22,23},{23,20},{2... | collective-permute-start | bytes 3170312 | tf_op jit(solution)/shard_map/ppermute | solution.py:266
  7.9 2.5 %collective-permute-start.6 = (f32[1032,256]{1,0:T(8,128)S(1)}, f32[1032,256]{1,0:T(8,128)}, u32[]{:S(2)}, u32[]{:S(2)}) collective-permute-start(f32[1032,256]{1,0:T(8,128)S(1)} %select_maximum_fusion.refs_0_), channel_id=1, source_target_pairs={{0,3},{1,0},{2,1},{3,2},{4,7},{5,4},{6,5},{7,6},{8,11},{9,8},{10,9... | collective-permute-start | bytes 3170312 | tf_op jit(solution)/shard_map/ppermute | solution.py:266
  10.5 16.1 %collective-permute-done.1.refs_2_ = f32[1032,256]{1,0:T(8,128)S(1)} collective-permute-done((f32[1032,256]{1,0:T(8,128)S(1)}, f32[1032,256]{1,0:T(8,128)S(1)}, u32[]{:S(2)}, u32[]{:S(2)}) %collective-permute-start.1) | collective-permute-done | bytes 1056800 | tf_op jit(solution)/shard_map/ppermute | solution.py:266
  26.5 3.1 %collective-permute-start.3 = (f32[1032,256]{1,0:T(8,128)S(1)}, f32[1032,256]{1,0:T(8,128)}, u32[]{:S(2)}, u32[]{:S(2)}) collective-permute-start(f32[1032,256]{1,0:T(8,128)S(1)} %collective-permute-done.1.refs_2_), channel_id=1, source_target_pairs={{20,4},{21,5},{22,6},{23,7},{28,12},{29,13},{30,14},{31,15},{4,20}... | collective-permute-start | bytes 3170312 | tf_op jit(solution)/shard_map/ppermute | solution.py:266
  29.7 1.6 %collective-permute-start.2 = (f32[1032,256]{1,0:T(8,128)S(1)}, f32[1032,256]{1,0:T(8,128)}, u32[]{:S(2)}, u32[]{:S(2)}) collective-permute-start(f32[1032,256]{1,0:T(8,128)S(1)} %collective-permute-done.refs_1_), channel_id=1, source_target_pairs={{8,0},{9,1},{10,2},{11,3},{0,8},{1,9},{2,10},{3,11},{24,16},{25,17... | collective-permute-start | bytes 3170312 | tf_op jit(solution)/shard_map/ppermute | solution.py:266
  31.3 1.3 %dynamic_slice.11 = s32[1,1]{1,0:T(1,128)} dynamic-slice(s32[8,4]{1,0:T(8,128)} %constant.33.clone, s32[]{:T(128)S(6)} %select_n.30, s32[]{:T(128)S(6)} %select_n.31), dynamic_slice_sizes={1,1} | dynamic-slice | bytes 12 | tf_op jit(solution)/shard_map/dynamic_slice | solution.py:259
  33.9 1.3 %dynamic_slice.10 = s32[1,1]{1,0:T(1,128)} dynamic-slice(s32[8,4]{1,0:T(8,128)} %constant.32.clone, s32[]{:T(128)S(6)} %select_n.30, s32[]{:T(128)S(6)} %select_n.31), dynamic_slice_sizes={1,1} | dynamic-slice | bytes 12 | tf_op jit(solution)/shard_map/dynamic_slice | solution.py:259
  35.8 1.4 %broadcast_select_fusion = f32[1032,256]{1,0:T(8,128)S(1)} fusion(f32[1032,256]{1,0:T(8,128)S(1)} %collective-permute-done.refs_1_, pred[]{:T(512)} %bitcast.1, f32[1,64]{1,0:T(1,128)S(1)} %reshape.9, f32[1024,256]{1,0:T(8,128)} %param.6), kind=kLoop, calls=%fused_computation.3 | loop fusion | flops 1056768 | bytes 3162369 | tf_op jit(solution)/shard_map/jit(_where)/select_n | solution.py:263
  37.2 0.6 collective-permute-start.4
  37.8 0.0 collective-permute-done.7.refs_8_
  37.8 1.3 %collective-permute-start.9 = (f32[1032,256]{1,0:T(8,128)}, f32[1032,256]{1,0:T(8,128)S(1)}, u32[]{:S(2)}, u32[]{:S(2)}) collective-permute-start(f32[1032,256]{1,0:T(8,128)} %collective-permute-done.7.refs_8_), channel_id=1, source_target_pairs={{16,17},{17,18},{18,19},{19,16},{20,21},{21,22},{22,23},{23,20},{1... | collective-permute-start | bytes 3170312 | tf_op jit(solution)/shard_map/ppermute | solution.py:266
  39.1 1.3 %collective-permute-start.8 = (f32[1032,256]{1,0:T(8,128)}, f32[1032,256]{1,0:T(8,128)S(1)}, u32[]{:S(2)}, u32[]{:S(2)}) collective-permute-start(f32[1032,256]{1,0:T(8,128)} %collective-permute-done.6.refs_7_), channel_id=1, source_target_pairs={{4,7},{5,4},{6,5},{7,6},{8,11},{9,8},{10,9},{11,10},{13,12},{14,13... | collective-permute-start | bytes 3170312 | tf_op jit(solution)/shard_map/ppermute | solution.py:266
  40.4 9.1 %collective-permute-done.3.refs_4_ = f32[1032,256]{1,0:T(8,128)} collective-permute-done((f32[1032,256]{1,0:T(8,128)S(1)}, f32[1032,256]{1,0:T(8,128)}, u32[]{:S(2)}, u32[]{:S(2)}) %collective-permute-start.3) | collective-permute-done | bytes 1056800 | tf_op jit(solution)/shard_map/ppermute | solution.py:266
  49.5 1.5 %select_select_fusion = f32[1032,256]{1,0:T(8,128)S(1)} fusion(f32[1032,256]{1,0:T(8,128)} %collective-permute-done.3.refs_4_, f32[1032,256]{1,0:T(8,128)} %collective-permute-done.2.refs_3_, f32[1032,256]{1,0:T(8,128)S(1)} %collective-permute-done.1.refs_2_, pred[]{:T(512)} %bitcast.3, pred[]{:T(512)} %bitcast.2), kind=kLoop, calls=%fused_computation.2 | loop fusion | flops 528384 | bytes 4227074 | tf_op jit(solution)/shard_map/jit(_where)/select_n | solution.py:263
  51.0 0.1 collective-permute-start.5
  51.1 0.7 dynamic-slice_bitcast_fusion.info_ref
  51.8 17.1 %collective-permute-done.9.refs_10_ = f32[1032,256]{1,0:T(8,128)S(1)} collective-permute-done((f32[1032,256]{1,0:T(8,128)}, f32[1032,256]{1,0:T(8,128)S(1)}, u32[]{:S(2)}, u32[]{:S(2)}) %collective-permute-start.9) | collective-permute-done | bytes 1056800 | tf_op jit(solution)/shard_map/ppermute | solution.py:266
  68.9 10.3 %shard_map.55 = f32[1024,2048]{1,0:T(8,128)} custom-call(s32[10]{0:T(128)S(1)} %dynamic-slice_bitcast_fusion.info_ref, f32[1032,256]{1,0:T(8,128)S(1)} %select_maximum_fusion.refs_0_, f32[1032,256]{1,0:T(8,128)S(1)} %collective-permute-done.refs_1_, f32[1032,256]{1,0:T(8,128)S(1)} %collective-permute-done.1.refs_2_, ...), custom_call_target="tpu_custom_call" | custom-call | flops 1000000000 | bytes 20971520 | tf_op jit(solution)/shard_map/pallas_call | solution.py:275
  (6 shorter events, 0.0 us)
Async XLA Ops:
  2.2 24.4 %collective-permute-start.1 = (f32[1032,256]{1,0:T(8,128)S(1)}, f32[1032,256]{1,0:T(8,128)S(1)}, u32[]{:S(2)}, u32[]{:S(2)}) collective-permute-start(f32[1032,256]{1,0:T(8,128)S(1)} %select_maximum_fusion.refs_0_), channel_id=1, source_target_pairs={{8,0},{9,1},{10,2},{11,3},{12,4},{13,5},{14,6},{15,7},{0,8},{1,9},... | collective-permute-start | bytes 3170312 | tf_op jit(solution)/shard_map/ppermute | solution.py:266
  2.2 27.4 %collective-permute-start = (f32[1032,256]{1,0:T(8,128)S(1)}, f32[1032,256]{1,0:T(8,128)S(1)}, u32[]{:S(2)}, u32[]{:S(2)}) collective-permute-start(f32[1032,256]{1,0:T(8,128)S(1)} %select_maximum_fusion.refs_0_), channel_id=1, source_target_pairs={{16,0},{17,1},{18,2},{19,3},{20,4},{21,5},{22,6},{23,7},{24,8},{25... | collective-permute-start | bytes 3170312 | tf_op jit(solution)/shard_map/ppermute | solution.py:266
  3.7 34.1 %collective-permute-start.7 = (f32[1032,256]{1,0:T(8,128)S(1)}, f32[1032,256]{1,0:T(8,128)}, u32[]{:S(2)}, u32[]{:S(2)}) collective-permute-start(f32[1032,256]{1,0:T(8,128)S(1)} %select_maximum_fusion.refs_0_), channel_id=1, source_target_pairs={{16,17},{17,18},{18,19},{19,16},{20,21},{21,22},{22,23},{23,20},{2... | collective-permute-start | bytes 3170312 | tf_op jit(solution)/shard_map/ppermute | solution.py:266
  7.9 31.2 %collective-permute-start.6 = (f32[1032,256]{1,0:T(8,128)S(1)}, f32[1032,256]{1,0:T(8,128)}, u32[]{:S(2)}, u32[]{:S(2)}) collective-permute-start(f32[1032,256]{1,0:T(8,128)S(1)} %select_maximum_fusion.refs_0_), channel_id=1, source_target_pairs={{0,3},{1,0},{2,1},{3,2},{4,7},{5,4},{6,5},{7,6},{8,11},{9,8},{10,9... | collective-permute-start | bytes 3170312 | tf_op jit(solution)/shard_map/ppermute | solution.py:266
  26.5 23.0 %collective-permute-start.3 = (f32[1032,256]{1,0:T(8,128)S(1)}, f32[1032,256]{1,0:T(8,128)}, u32[]{:S(2)}, u32[]{:S(2)}) collective-permute-start(f32[1032,256]{1,0:T(8,128)S(1)} %collective-permute-done.1.refs_2_), channel_id=1, source_target_pairs={{20,4},{21,5},{22,6},{23,7},{28,12},{29,13},{30,14},{31,15},{4,20}... | collective-permute-start | bytes 3170312 | tf_op jit(solution)/shard_map/ppermute | solution.py:266
  29.7 19.8 %collective-permute-start.2 = (f32[1032,256]{1,0:T(8,128)S(1)}, f32[1032,256]{1,0:T(8,128)}, u32[]{:S(2)}, u32[]{:S(2)}) collective-permute-start(f32[1032,256]{1,0:T(8,128)S(1)} %collective-permute-done.refs_1_), channel_id=1, source_target_pairs={{8,0},{9,1},{10,2},{11,3},{0,8},{1,9},{2,10},{3,11},{24,16},{25,17... | collective-permute-start | bytes 3170312 | tf_op jit(solution)/shard_map/ppermute | solution.py:266
  37.2 31.7 %collective-permute-start.4 = (f32[1032,256]{1,0:T(8,128)S(1)}, f32[1032,256]{1,0:T(8,128)S(1)}, u32[]{:S(2)}, u32[]{:S(2)}) collective-permute-start(f32[1032,256]{1,0:T(8,128)S(1)} %broadcast_select_fusion), channel_id=1, source_target_pairs={{4,0},{5,1},{6,2},{7,3},{0,4},{1,5},{2,6},{3,7},{12,8},{13,9},{14,... | collective-permute-start | bytes 3170312 | tf_op jit(solution)/shard_map/ppermute | solution.py:266
  37.8 31.1 %collective-permute-start.9 = (f32[1032,256]{1,0:T(8,128)}, f32[1032,256]{1,0:T(8,128)S(1)}, u32[]{:S(2)}, u32[]{:S(2)}) collective-permute-start(f32[1032,256]{1,0:T(8,128)} %collective-permute-done.7.refs_8_), channel_id=1, source_target_pairs={{16,17},{17,18},{18,19},{19,16},{20,21},{21,22},{22,23},{23,20},{1... | collective-permute-start | bytes 3170312 | tf_op jit(solution)/shard_map/ppermute | solution.py:266
  39.1 29.8 %collective-permute-start.8 = (f32[1032,256]{1,0:T(8,128)}, f32[1032,256]{1,0:T(8,128)S(1)}, u32[]{:S(2)}, u32[]{:S(2)}) collective-permute-start(f32[1032,256]{1,0:T(8,128)} %collective-permute-done.6.refs_7_), channel_id=1, source_target_pairs={{4,7},{5,4},{6,5},{7,6},{8,11},{9,8},{10,9},{11,10},{13,12},{14,13... | collective-permute-start | bytes 3170312 | tf_op jit(solution)/shard_map/ppermute | solution.py:266
  51.0 17.9 %collective-permute-start.5 = (f32[1032,256]{1,0:T(8,128)S(1)}, f32[1032,256]{1,0:T(8,128)S(1)}, u32[]{:S(2)}, u32[]{:S(2)}) collective-permute-start(f32[1032,256]{1,0:T(8,128)S(1)} %select_select_fusion), channel_id=1, source_target_pairs={{4,0},{5,1},{6,2},{7,3},{0,4},{1,5},{2,6},{3,7},{12,8},{13,9},{14,... | collective-permute-start | bytes 3170312 | tf_op jit(solution)/shard_map/ppermute | solution.py:266

commit v3 on v2

--- a/solution.py
+++ b/solution.py
@@ -234,6 +234,18 @@
         out_copy(part).wait()
 
 
+def passed_on(bufs):
+    hbm = pl.BlockSpec(memory_space=pl.ANY)
+    return pl.pallas_call(
+        lambda *refs: None,
+        out_shape=[jax.ShapeDtypeStruct(buf.shape, buf.dtype) for buf in bufs],
+        in_specs=[hbm] * len(bufs),
+        out_specs=[hbm] * len(bufs),
+        input_output_aliases={i: i for i in range(len(bufs))},
+        cost_estimate=pl.CostEstimate(flops=10**11, bytes_accessed=0, transcendentals=0),
+    )(*bufs)
+
+
 def local(p_cols, p_data):
     n_row, n_col = lax.axis_size("row"), lax.axis_size("col")
     ratio = n_row // n_col
@@ -267,6 +279,7 @@
         return bufs
 
     right_bufs, left_bufs = carry(right_perms), carry(left_perms)
+    left_bufs[3:] = passed_on(left_bufs[3:])
     out_shape = jax.ShapeDtypeStruct((rows, rb * ratio * BS), jnp.float32)
     smem = pl.BlockSpec(memory_space=pltpu.SMEM)
     hbm = pl.BlockSpec(memory_space=pl.ANY)

time: 80.1 us -> 79.6 us (level)
  waiting for transfers between devices: 42.3 us -> 33.4 us
  starting transfers between devices: 16.3 us -> 21.8 us
  other arithmetic: 4.84 us -> 6.86 us
  Pallas kernels: 10.3 us -> 11.6 us
    ppermute x10, waiting for transfers between devices: 42.3 us -> 33.4 us  [carry(): lax.ppermute(value, ('row', 'col'), [(s[0] * n_col + s[1], d[0] * n_col +...]
    ppermute x10, starting transfers between devices: 16.3 us -> 21.8 us  [carry(): lax.ppermute(value, ('row', 'col'), [(s[0] * n_col + s[1], d[0] * n_col +...]
    select_n x2, other arithmetic: 2.86 us -> 4.88 us  [carry(): value = jnp.where(pick == other, bufs[other], value)]
    pallas_call x1, Pallas kernels: 10.3 us -> 11.6 us  [local(): pl.pallas_call(functools.partial(product_kernel, slots, n_row, ratio, rb,...]
  transfers between devices with their start and end apart: 10 -> 10, of which waited for: 3 -> 4; matrix products, arithmetic and copies ran while one was open for 8% -> 10% of each run, Pallas kernels for 0% -> 0%
where the time goes in v3:
time: 79.6 us; the launch traced here: 79.1 us
  waiting for transfers between devices  33.4 us (42%)
  starting transfers between devices  21.8 us (27%)
  Pallas kernels  11.6 us (15%)
  other arithmetic  6.86 us (9%)
  local copies, waits for them, and re-layouts  3.41 us (4%)
  between operations  2.02 us (3%)
    ppermute x10, waiting for transfers between devices, carry(): lax.ppermute(value, ('row', 'col'), [(s[0] * n_col + s[1], d[0] * n_col +...  33.4 us
    ppermute x10, starting transfers between devices, carry(): lax.ppermute(value, ('row', 'col'), [(s[0] * n_col + s[1], d[0] * n_col +...  21.8 us
    pallas_call x1, Pallas kernels, local(): pl.pallas_call(functools.partial(product_kernel, slots, n_row, ratio, rb,...  11.6 us
    select_n x2, other arithmetic, carry(): value = jnp.where(pick == other, bufs[other], value)  4.88 us
    dynamic_slice x2, local copies, waits for them, and re-layouts, carry(): pick = jnp.asarray(picks)[row_id, col_id]  2.55 us
  transfers between devices with their start and end apart: 10, of which 4 were waited for; matrix products, arithmetic and copies ran while one was open for 10% of the time, Pallas kernels for 0%

profile of v3, /device:TPU:3, one launch (start us, length us, event | category | flops | bytes accessed | tf_op | source)
XLA Modules:
  0.0 79.1 jit_solution(14886417501534878664)
XLA Ops:
  0.0 0.7 convert_element_type.5
  0.7 0.1 copy.9
  0.8 0.1 reshape.9
  0.9 1.3 %select_maximum_fusion.refs_0_ = f32[1032,256]{1,0:T(8,128)S(1)} fusion(f32[1,64]{1,0:T(1,128)S(1)} %reshape.9, f32[1024,256]{1,0:T(8,128)} %param.6), kind=kLoop, calls=%fused_computation | loop fusion | flops 792576 | bytes 2105600 | tf_op jit(solution)/shard_map/concatenate | solution.py:261
  2.2 0.1 collective-permute-start.1
  2.2 1.5 %collective-permute-start = (f32[1032,256]{1,0:T(8,128)S(1)}, f32[1032,256]{1,0:T(8,128)S(1)}, u32[]{:S(2)}, u32[]{:S(2)}) collective-permute-start(f32[1032,256]{1,0:T(8,128)S(1)} %select_maximum_fusion.refs_0_), channel_id=1, source_target_pairs={{16,0},{17,1},{18,2},{19,3},{20,4},{21,5},{22,6},{23,7},{24,8},{25... | collective-permute-start | bytes 3170312 | tf_op jit(solution)/shard_map/ppermute | solution.py:278
  3.7 4.2 %collective-permute-start.7 = (f32[1032,256]{1,0:T(8,128)S(1)}, f32[1032,256]{1,0:T(8,128)}, u32[]{:S(2)}, u32[]{:S(2)}) collective-permute-start(f32[1032,256]{1,0:T(8,128)S(1)} %select_maximum_fusion.refs_0_), channel_id=1, source_target_pairs={{16,17},{17,18},{18,19},{19,16},{20,21},{21,22},{22,23},{23,20},{2... | collective-permute-start | bytes 3170312 | tf_op jit(solution)/shard_map/ppermute | solution.py:278
  7.9 2.5 %collective-permute-start.6 = (f32[1032,256]{1,0:T(8,128)S(1)}, f32[1032,256]{1,0:T(8,128)}, u32[]{:S(2)}, u32[]{:S(2)}) collective-permute-start(f32[1032,256]{1,0:T(8,128)S(1)} %select_maximum_fusion.refs_0_), channel_id=1, source_target_pairs={{0,3},{1,0},{2,1},{3,2},{4,7},{5,4},{6,5},{7,6},{8,11},{9,8},{10,9... | collective-permute-start | bytes 3170312 | tf_op jit(solution)/shard_map/ppermute | solution.py:278
  10.5 16.1 %collective-permute-done.1.refs_2_ = f32[1032,256]{1,0:T(8,128)S(1)} collective-permute-done((f32[1032,256]{1,0:T(8,128)S(1)}, f32[1032,256]{1,0:T(8,128)S(1)}, u32[]{:S(2)}, u32[]{:S(2)}) %collective-permute-start.1) | collective-permute-done | bytes 1056800 | tf_op jit(solution)/shard_map/ppermute | solution.py:278
  26.5 3.1 %collective-permute-start.3 = (f32[1032,256]{1,0:T(8,128)S(1)}, f32[1032,256]{1,0:T(8,128)}, u32[]{:S(2)}, u32[]{:S(2)}) collective-permute-start(f32[1032,256]{1,0:T(8,128)S(1)} %collective-permute-done.1.refs_2_), channel_id=1, source_target_pairs={{20,4},{21,5},{22,6},{23,7},{28,12},{29,13},{30,14},{31,15},{4,20}... | collective-permute-start | bytes 3170312 | tf_op jit(solution)/shard_map/ppermute | solution.py:278
  29.7 0.0 collective-permute-done.refs_1_
  29.7 1.6 %collective-permute-start.2 = (f32[1032,256]{1,0:T(8,128)S(1)}, f32[1032,256]{1,0:T(8,128)}, u32[]{:S(2)}, u32[]{:S(2)}) collective-permute-start(f32[1032,256]{1,0:T(8,128)S(1)} %collective-permute-done.refs_1_), channel_id=1, source_target_pairs={{8,0},{9,1},{10,2},{11,3},{0,8},{1,9},{2,10},{3,11},{24,16},{25,17... | collective-permute-start | bytes 3170312 | tf_op jit(solution)/shard_map/ppermute | solution.py:278
  31.3 1.3 %dynamic_slice.11 = s32[1,1]{1,0:T(1,128)} dynamic-slice(s32[8,4]{1,0:T(8,128)} %constant.33.clone, s32[]{:T(128)S(6)} %select_n.30, s32[]{:T(128)S(6)} %select_n.31), dynamic_slice_sizes={1,1} | dynamic-slice | bytes 12 | tf_op jit(solution)/shard_map/dynamic_slice | solution.py:271
  33.9 1.3 %dynamic_slice.10 = s32[1,1]{1,0:T(1,128)} dynamic-slice(s32[8,4]{1,0:T(8,128)} %constant.32.clone, s32[]{:T(128)S(6)} %select_n.30, s32[]{:T(128)S(6)} %select_n.31), dynamic_slice_sizes={1,1} | dynamic-slice | bytes 12 | tf_op jit(solution)/shard_map/dynamic_slice | solution.py:271
  35.8 0.7 dynamic-slice_bitcast_fusion.info_ref
  36.5 1.3 %collective-permute-start.9 = (f32[1032,256]{1,0:T(8,128)}, f32[1032,256]{1,0:T(8,128)}, u32[]{:S(2)}, u32[]{:S(2)}) collective-permute-start(f32[1032,256]{1,0:T(8,128)} %collective-permute-done.7.refs_8_), channel_id=1, source_target_pairs={{16,17},{17,18},{18,19},{19,16},{20,21},{21,22},{22,23},{23,20},{1... | collective-permute-start | bytes 3170312 | tf_op jit(solution)/shard_map/ppermute | solution.py:278
  37.8 0.4 collective-permute-done.6.refs_7_
  38.2 1.3 %collective-permute-start.8 = (f32[1032,256]{1,0:T(8,128)}, f32[1032,256]{1,0:T(8,128)}, u32[]{:S(2)}, u32[]{:S(2)}) collective-permute-start(f32[1032,256]{1,0:T(8,128)} %collective-permute-done.6.refs_7_), channel_id=1, source_target_pairs={{4,7},{5,4},{6,5},{7,6},{8,11},{9,8},{10,9},{11,10},{13,12},{14,13... | collective-permute-start | bytes 3170312 | tf_op jit(solution)/shard_map/ppermute | solution.py:278
  39.5 2.3 %broadcast_select_fusion = f32[1032,256]{1,0:T(8,128)} fusion(f32[1032,256]{1,0:T(8,128)S(1)} %collective-permute-done.refs_1_, pred[]{:T(512)} %bitcast.1, f32[1,64]{1,0:T(1,128)S(1)} %reshape.9, f32[1024,256]{1,0:T(8,128)} %param.6), kind=kLoop, calls=%fused_computation.3 | loop fusion | flops 1056768 | bytes 3162369 | tf_op jit(solution)/shard_map/jit(_where)/select_n | solution.py:275
  41.8 6.2 %collective-permute-start.4 = (f32[1032,256]{1,0:T(8,128)}, f32[1032,256]{1,0:T(8,128)}, u32[]{:S(2)}, u32[]{:S(2)}) collective-permute-start(f32[1032,256]{1,0:T(8,128)} %broadcast_select_fusion), channel_id=1, source_target_pairs={{4,0},{5,1},{6,2},{7,3},{0,4},{1,5},{2,6},{3,7},{12,8},{13,9},{14,... | collective-permute-start | bytes 3170312 | tf_op jit(solution)/shard_map/ppermute | solution.py:278
  48.0 1.5 %collective-permute-done.3.refs_4_ = f32[1032,256]{1,0:T(8,128)} collective-permute-done((f32[1032,256]{1,0:T(8,128)S(1)}, f32[1032,256]{1,0:T(8,128)}, u32[]{:S(2)}, u32[]{:S(2)}) %collective-permute-start.3) | collective-permute-done | bytes 1056800 | tf_op jit(solution)/shard_map/ppermute | solution.py:278
  49.5 2.5 %select_select_fusion = f32[1032,256]{1,0:T(8,128)} fusion(f32[1032,256]{1,0:T(8,128)} %collective-permute-done.3.refs_4_, f32[1032,256]{1,0:T(8,128)} %collective-permute-done.2.refs_3_, f32[1032,256]{1,0:T(8,128)S(1)} %collective-permute-done.1.refs_2_, pred[]{:T(512)} %bitcast.3, pred[]{:T(512)} %bitcast.2), kind=kLoop, calls=%fused_computation.2 | loop fusion | flops 528384 | bytes 4227074 | tf_op jit(solution)/shard_map/jit(_where)/select_n | solution.py:275
  52.1 15.4 %collective-permute-done.9.refs_1_ = f32[1032,256]{1,0:T(8,128)} collective-permute-done((f32[1032,256]{1,0:T(8,128)}, f32[1032,256]{1,0:T(8,128)}, u32[]{:S(2)}, u32[]{:S(2)}) %collective-permute-start.9) | collective-permute-done | bytes 1056800 | tf_op jit(solution)/shard_map/ppermute | solution.py:278
  67.5 11.6 %shard_map.56 = f32[1024,2048]{1,0:T(8,128)} custom-call(s32[10]{0:T(128)S(1)} %dynamic-slice_bitcast_fusion.info_ref, f32[1032,256]{1,0:T(8,128)S(1)} %select_maximum_fusion.refs_0_, f32[1032,256]{1,0:T(8,128)S(1)} %collective-permute-done.refs_1_, f32[1032,256]{1,0:T(8,128)S(1)} %collective-permute-done.1.refs_2_, ...), custom_call_target="tpu_custom_call" | custom-call | flops 1000000000 | bytes 20971520 | tf_op jit(solution)/shard_map/pallas_call | solution.py:288
  (7 shorter events, 0.0 us)
Async XLA Ops:
  2.2 24.4 %collective-permute-start.1 = (f32[1032,256]{1,0:T(8,128)S(1)}, f32[1032,256]{1,0:T(8,128)S(1)}, u32[]{:S(2)}, u32[]{:S(2)}) collective-permute-start(f32[1032,256]{1,0:T(8,128)S(1)} %select_maximum_fusion.refs_0_), channel_id=1, source_target_pairs={{8,0},{9,1},{10,2},{11,3},{12,4},{13,5},{14,6},{15,7},{0,8},{1,9},... | collective-permute-start | bytes 3170312 | tf_op jit(solution)/shard_map/ppermute | solution.py:278
  2.2 27.4 %collective-permute-start = (f32[1032,256]{1,0:T(8,128)S(1)}, f32[1032,256]{1,0:T(8,128)S(1)}, u32[]{:S(2)}, u32[]{:S(2)}) collective-permute-start(f32[1032,256]{1,0:T(8,128)S(1)} %select_maximum_fusion.refs_0_), channel_id=1, source_target_pairs={{16,0},{17,1},{18,2},{19,3},{20,4},{21,5},{22,6},{23,7},{24,8},{25... | collective-permute-start | bytes 3170312 | tf_op jit(solution)/shard_map/ppermute | solution.py:278
  3.7 32.8 %collective-permute-start.7 = (f32[1032,256]{1,0:T(8,128)S(1)}, f32[1032,256]{1,0:T(8,128)}, u32[]{:S(2)}, u32[]{:S(2)}) collective-permute-start(f32[1032,256]{1,0:T(8,128)S(1)} %select_maximum_fusion.refs_0_), channel_id=1, source_target_pairs={{16,17},{17,18},{18,19},{19,16},{20,21},{21,22},{22,23},{23,20},{2... | collective-permute-start | bytes 3170312 | tf_op jit(solution)/shard_map/ppermute | solution.py:278
  7.9 30.3 %collective-permute-start.6 = (f32[1032,256]{1,0:T(8,128)S(1)}, f32[1032,256]{1,0:T(8,128)}, u32[]{:S(2)}, u32[]{:S(2)}) collective-permute-start(f32[1032,256]{1,0:T(8,128)S(1)} %select_maximum_fusion.refs_0_), channel_id=1, source_target_pairs={{0,3},{1,0},{2,1},{3,2},{4,7},{5,4},{6,5},{7,6},{8,11},{9,8},{10,9... | collective-permute-start | bytes 3170312 | tf_op jit(solution)/shard_map/ppermute | solution.py:278
  26.5 23.0 %collective-permute-start.3 = (f32[1032,256]{1,0:T(8,128)S(1)}, f32[1032,256]{1,0:T(8,128)}, u32[]{:S(2)}, u32[]{:S(2)}) collective-permute-start(f32[1032,256]{1,0:T(8,128)S(1)} %collective-permute-done.1.refs_2_), channel_id=1, source_target_pairs={{20,4},{21,5},{22,6},{23,7},{28,12},{29,13},{30,14},{31,15},{4,20}... | collective-permute-start | bytes 3170312 | tf_op jit(solution)/shard_map/ppermute | solution.py:278
  29.7 19.8 %collective-permute-start.2 = (f32[1032,256]{1,0:T(8,128)S(1)}, f32[1032,256]{1,0:T(8,128)}, u32[]{:S(2)}, u32[]{:S(2)}) collective-permute-start(f32[1032,256]{1,0:T(8,128)S(1)} %collective-permute-done.refs_1_), channel_id=1, source_target_pairs={{8,0},{9,1},{10,2},{11,3},{0,8},{1,9},{2,10},{3,11},{24,16},{25,17... | collective-permute-start | bytes 3170312 | tf_op jit(solution)/shard_map/ppermute | solution.py:278
  36.5 31.0 %collective-permute-start.9 = (f32[1032,256]{1,0:T(8,128)}, f32[1032,256]{1,0:T(8,128)}, u32[]{:S(2)}, u32[]{:S(2)}) collective-permute-start(f32[1032,256]{1,0:T(8,128)} %collective-permute-done.7.refs_8_), channel_id=1, source_target_pairs={{16,17},{17,18},{18,19},{19,16},{20,21},{21,22},{22,23},{23,20},{1... | collective-permute-start | bytes 3170312 | tf_op jit(solution)/shard_map/ppermute | solution.py:278
  38.2 29.3 %collective-permute-start.8 = (f32[1032,256]{1,0:T(8,128)}, f32[1032,256]{1,0:T(8,128)}, u32[]{:S(2)}, u32[]{:S(2)}) collective-permute-start(f32[1032,256]{1,0:T(8,128)} %collective-permute-done.6.refs_7_), channel_id=1, source_target_pairs={{4,7},{5,4},{6,5},{7,6},{8,11},{9,8},{10,9},{11,10},{13,12},{14,13... | collective-permute-start | bytes 3170312 | tf_op jit(solution)/shard_map/ppermute | solution.py:278
  41.8 25.7 %collective-permute-start.4 = (f32[1032,256]{1,0:T(8,128)}, f32[1032,256]{1,0:T(8,128)}, u32[]{:S(2)}, u32[]{:S(2)}) collective-permute-start(f32[1032,256]{1,0:T(8,128)} %broadcast_select_fusion), channel_id=1, source_target_pairs={{4,0},{5,1},{6,2},{7,3},{0,4},{1,5},{2,6},{3,7},{12,8},{13,9},{14,... | collective-permute-start | bytes 3170312 | tf_op jit(solution)/shard_map/ppermute | solution.py:278
  52.1 15.4 %collective-permute-start.5 = (f32[1032,256]{1,0:T(8,128)}, f32[1032,256]{1,0:T(8,128)}, u32[]{:S(2)}, u32[]{:S(2)}) collective-permute-start(f32[1032,256]{1,0:T(8,128)} %select_select_fusion), channel_id=1, source_target_pairs={{4,0},{5,1},{6,2},{7,3},{0,4},{1,5},{2,6},{3,7},{12,8},{13,9},{14,... | collective-permute-start | bytes 3170312 | tf_op jit(solution)/shard_map/ppermute | solution.py:278

commit v4 on v2

--- a/solution.py
+++ b/solution.py
@@ -58,27 +58,20 @@
             (0, [(((r + ratio * c + step) % n_row, c), (r, c)) for r, c in everyone if (ratio * c + step) % n_row])
             for step in range(STEPS)
         ]
-    along_y = [((r ^ 4, c), (r, c)) for r, c in everyone]
-    along_x = [((r ^ 2, c), (r, c)) for r, c in everyone]
-    even = [((r ^ 2, c), (r, c)) for r, c in everyone if r % 2 == 0]
-    odd = [((r ^ 4, c), (r, c)) for r, c in everyone if r % 2 == 1]
-    perms = [(0, along_y), (0, along_x), (1, even), (2, odd)]
-    held = carry_out(perms, n_row, n_col)
-    swap = [((r ^ 1, c), (r, c)) for r, c in everyone]
-    for buffers in ((0, 1), (2, 3, 4)):
-        choice = {}
-        for r, c in everyone:
-            needs = [((r ^ 1) + 2 * c + step) % 8 for step in range(STEPS)]
-            choice[r, c] = [b for b in buffers if held[b].get((r, c)) in [(k, c) for k in needs]][0]
-        perms.append((choice, swap))
-    return perms
+    first = [(((r + 2 * c) % 8, c), (r, c)) for r, c in everyone if c != 0]
+    first += [((r + 1, 0), (r, 0)) for r in range(0, 8, 2)]
+    second = [(((r + 2 * c + 2) % 8, c), (r, c)) for r, c in everyone if c != 3]
+    second += [((r ^ 1, 3), (r, 3)) for r in range(8)]
+    last = [(((r - 1 + 2 * c + 4) % 8, c), (r, c)) for r, c in everyone if r % 2 == 1]
+    first_swap = [((r + 1, c), (r, c)) for r, c in everyone if r % 2 == 0 and c != 0]
+    second_swap = [((r ^ 1, c), (r, c)) for r, c in everyone if c != 3]
+    return [(0, first), (0, second), (0, last), (1, first_swap), (2, second_swap)]
 
 
 def carry_out(perms, n_row, n_col):
     held = [{(r, c): (r, c) for r in range(n_row) for c in range(n_col)}]
     for source, pairs in perms:
-        pick = source.get if isinstance(source, dict) else lambda device: source
-        held.append({dst: held[pick(src)][src] for src, dst in pairs})
+        held.append({dst: held[source][src] for src, dst in pairs})
     return held
 
 
@@ -248,25 +241,14 @@
     cols = jnp.pad(p_cols.astype(jnp.float32).reshape(1, -1), ((0, EXTRA - 1), (0, width - rb * w)))
     own = jnp.concatenate([p_data, cols], axis=0)
 
-    def permute(value, pairs):
-        return lax.ppermute(value, ("row", "col"), [(s[0] * n_col + s[1], d[0] * n_col + d[1]) for s, d in pairs])
-
     def carry(perms):
         bufs = [own]
         for source, pairs in perms:
-            if isinstance(source, dict):
-                picks = np.array([[source[r, c] for c in range(n_col)] for r in range(n_row)], np.int32)
-                pick = jnp.asarray(picks)[row_id, col_id]
-                first, *others = sorted(set(source.values()))
-                value = bufs[first]
-                for other in others:
-                    value = jnp.where(pick == other, bufs[other], value)
-            else:
-                value = bufs[source]
-            bufs.append(lax.ppermute(value, ("row", "col"), [(s[0] * n_col + s[1], d[0] * n_col + d[1]) for s, d in pairs]))
+            flat = [(s[0] * n_col + s[1], d[0] * n_col + d[1]) for s, d in pairs]
+            bufs.append(lax.ppermute(bufs[source], ("row", "col"), flat))
         return bufs
 
-    right_bufs, left_bufs = carry(right_perms), carry(left_perms)
+    left_bufs, right_bufs = carry(left_perms), carry(right_perms)
     out_shape = jax.ShapeDtypeStruct((rows, rb * ratio * BS), jnp.float32)
     smem = pl.BlockSpec(memory_space=pltpu.SMEM)
     hbm = pl.BlockSpec(memory_space=pl.ANY)

time: 80.1 us -> 81.7 us (1.020)
  the two profiles are of different devices: /device:TPU:3 before, /device:TPU:27 now
where the time goes in v4:
time: 81.7 us; the launch traced here: 81.9 us
  waiting for transfers between devices  52.1 us (64%)
  starting transfers between devices  15.1 us (18%)
  Pallas kernels  11.7 us (14%)
  other arithmetic  1.98 us (2%)
  local copies, waits for them, and re-layouts  0.86 us (1%)
    ppermute x9, waiting for transfers between devices, carry(): bufs.append(lax.ppermute(bufs[source], ('row', 'col'), flat))  52.1 us
    ppermute x9, starting transfers between devices, carry(): bufs.append(lax.ppermute(bufs[source], ('row', 'col'), flat))  15.1 us
    pallas_call x1, Pallas kernels, local(): pl.pallas_call(functools.partial(product_kernel, slots, n_row, ratio, rb,...  11.7 us
  transfers between devices with their start and end apart: 9, of which 4 were waited for; matrix products, arithmetic and copies ran while one was open for 1% of the time, Pallas kernels for 0%

profile of v4, /device:TPU:27, one launch (start us, length us, event | category | flops | bytes accessed | tf_op | source)
XLA Modules:
  0.0 81.9 jit_solution(3371524250937571260)
XLA Ops:
  0.0 0.7 convert_element_type.5
  0.7 0.1 copy.5
  0.8 0.1 reshape.3
  0.9 1.3 %select_maximum_fusion.refs_0_ = f32[1032,256]{1,0:T(8,128)S(1)} fusion(f32[1,64]{1,0:T(1,128)S(1)} %reshape.3, f32[1024,256]{1,0:T(8,128)} %param.4), kind=kLoop, calls=%fused_computation | loop fusion | flops 792576 | bytes 2105600 | tf_op jit(solution)/shard_map/concatenate | solution.py:242
  2.2 2.7 %collective-permute-start.6 = (f32[1032,256]{1,0:T(8,128)S(1)}, f32[1032,256]{1,0:T(8,128)S(1)}, u32[]{:S(2)}, u32[]{:S(2)}) collective-permute-start(f32[1032,256]{1,0:T(8,128)S(1)} %select_maximum_fusion.refs_0_), channel_id=1, source_target_pairs={{16,17},{17,18},{18,19},{19,16},{20,21},{21,22},{22,23},{23,20},{2... | collective-permute-start | bytes 3170312 | tf_op jit(solution)/shard_map/ppermute | solution.py:248
  4.9 2.6 %collective-permute-start.5 = (f32[1032,256]{1,0:T(8,128)S(1)}, f32[1032,256]{1,0:T(8,128)S(1)}, u32[]{:S(2)}, u32[]{:S(2)}) collective-permute-start(f32[1032,256]{1,0:T(8,128)S(1)} %select_maximum_fusion.refs_0_), channel_id=1, source_target_pairs={{0,3},{1,0},{2,1},{3,2},{4,7},{5,4},{6,5},{7,6},{8,11},{9,8},{10,9... | collective-permute-start | bytes 3170312 | tf_op jit(solution)/shard_map/ppermute | solution.py:248
  7.5 0.1 collective-permute-start.1
  7.6 1.9 %collective-permute-start = (f32[1032,256]{1,0:T(8,128)S(1)}, f32[1032,256]{1,0:T(8,128)}, u32[]{:S(2)}, u32[]{:S(2)}) collective-permute-start(f32[1032,256]{1,0:T(8,128)S(1)} %select_maximum_fusion.refs_0_), channel_id=1, source_target_pairs={{9,1},{18,2},{27,3},{13,5},{22,6},{31,7},{17,9},{26,10},{3,11},{21... | collective-permute-start | bytes 3170312 | tf_op jit(solution)/shard_map/ppermute | solution.py:248
  9.5 1.3 %collective-permute-start.2 = (f32[1032,256]{1,0:T(8,128)S(1)}, f32[1032,256]{1,0:T(8,128)}, u32[]{:S(2)}, u32[]{:S(2)}) collective-permute-start(f32[1032,256]{1,0:T(8,128)S(1)} %select_maximum_fusion.refs_0_), channel_id=1, source_target_pairs={{16,4},{25,5},{2,6},{11,7},{24,12},{1,13},{10,14},{19,15},{0,20},{... | collective-permute-start | bytes 3170312 | tf_op jit(solution)/shard_map/ppermute | solution.py:248
  10.8 18.7 %collective-permute-done.6.refs_7_ = f32[1032,256]{1,0:T(8,128)S(1)} collective-permute-done((f32[1032,256]{1,0:T(8,128)S(1)}, f32[1032,256]{1,0:T(8,128)S(1)}, u32[]{:S(2)}, u32[]{:S(2)}) %collective-permute-start.6) | collective-permute-done | bytes 1056800 | tf_op jit(solution)/shard_map/ppermute | solution.py:248
  29.5 1.3 %collective-permute-start.8 = (f32[1032,256]{1,0:T(8,128)S(1)}, f32[1032,256]{1,0:T(8,128)}, u32[]{:S(2)}, u32[]{:S(2)}) collective-permute-start(f32[1032,256]{1,0:T(8,128)S(1)} %collective-permute-done.6.refs_7_), channel_id=1, source_target_pairs={{16,17},{17,18},{18,19},{19,16},{20,21},{21,22},{22,23},{23,20},{1... | collective-permute-start | bytes 3170312 | tf_op jit(solution)/shard_map/ppermute | solution.py:248
  30.8 0.0 collective-permute-done.5.refs_6_
  30.8 1.3 %collective-permute-start.7 = (f32[1032,256]{1,0:T(8,128)S(1)}, f32[1032,256]{1,0:T(8,128)}, u32[]{:S(2)}, u32[]{:S(2)}) collective-permute-start(f32[1032,256]{1,0:T(8,128)S(1)} %collective-permute-done.5.refs_6_), channel_id=1, source_target_pairs={{4,7},{5,4},{6,5},{7,6},{8,11},{9,8},{10,9},{11,10},{13,12},{14,13... | collective-permute-start | bytes 3170312 | tf_op jit(solution)/shard_map/ppermute | solution.py:248
  32.1 0.0 collective-permute-done.1.refs_2_
  32.1 1.6 %collective-permute-start.4 = (f32[1032,256]{1,0:T(8,128)}, f32[1032,256]{1,0:T(8,128)}, u32[]{:S(2)}, u32[]{:S(2)}) collective-permute-start(f32[1032,256]{1,0:T(8,128)} %collective-permute-done.1.refs_2_), channel_id=1, source_target_pairs={{4,0},{5,1},{6,2},{0,4},{1,5},{2,6},{12,8},{13,9},{14,10},{8,12},{... | collective-permute-start | bytes 3170312 | tf_op jit(solution)/shard_map/ppermute | solution.py:248
  33.8 11.6 %collective-permute-done.refs_1_ = f32[1032,256]{1,0:T(8,128)} collective-permute-done((f32[1032,256]{1,0:T(8,128)S(1)}, f32[1032,256]{1,0:T(8,128)}, u32[]{:S(2)}, u32[]{:S(2)}) %collective-permute-start) | collective-permute-done | bytes 1056800 | tf_op jit(solution)/shard_map/ppermute | solution.py:248
  45.3 2.3 %collective-permute-start.3 = (f32[1032,256]{1,0:T(8,128)}, f32[1032,256]{1,0:T(8,128)}, u32[]{:S(2)}, u32[]{:S(2)}) collective-permute-start(f32[1032,256]{1,0:T(8,128)} %collective-permute-done.refs_1_), channel_id=1, source_target_pairs={{5,1},{6,2},{7,3},{13,9},{14,10},{15,11},{21,17},{22,18},{23,19},{... | collective-permute-start | bytes 3170312 | tf_op jit(solution)/shard_map/ppermute | solution.py:248
  47.6 0.7 dynamic-slice_bitcast_fusion.info_ref
  48.3 0.0 collective-permute-done.2.refs_3_
  48.3 8.3 %collective-permute-done.8.refs_9_ = f32[1032,256]{1,0:T(8,128)} collective-permute-done((f32[1032,256]{1,0:T(8,128)S(1)}, f32[1032,256]{1,0:T(8,128)}, u32[]{:S(2)}, u32[]{:S(2)}) %collective-permute-start.8) | collective-permute-done | bytes 1056800 | tf_op jit(solution)/shard_map/ppermute | solution.py:248
  56.6 13.6 %collective-permute-done.7.refs_8_ = f32[1032,256]{1,0:T(8,128)} collective-permute-done((f32[1032,256]{1,0:T(8,128)S(1)}, f32[1032,256]{1,0:T(8,128)}, u32[]{:S(2)}, u32[]{:S(2)}) %collective-permute-start.7) | collective-permute-done | bytes 1056800 | tf_op jit(solution)/shard_map/ppermute | solution.py:248
  70.1 0.0 collective-permute-done.4.refs_5_
  70.1 0.0 collective-permute-done.3.refs_4_
  70.1 11.7 %shard_map.37 = f32[1024,2048]{1,0:T(8,128)} custom-call(s32[10]{0:T(128)S(1)} %dynamic-slice_bitcast_fusion.info_ref, f32[1032,256]{1,0:T(8,128)S(1)} %select_maximum_fusion.refs_0_, f32[1032,256]{1,0:T(8,128)} %collective-permute-done.refs_1_, f32[1032,256]{1,0:T(8,128)} %collective-permute-done.1.refs_2_, f32[1032,256]{1,0:T(8,128)} %collective-permute-done.2.refs_3_, ...), custom_call_target="tpu_custom_call" | custom-call | flops 1000000000 | bytes 20971520 | tf_op jit(solution)/shard_map/pallas_call | solution.py:257
Async XLA Ops:
  2.2 27.4 %collective-permute-start.6 = (f32[1032,256]{1,0:T(8,128)S(1)}, f32[1032,256]{1,0:T(8,128)S(1)}, u32[]{:S(2)}, u32[]{:S(2)}) collective-permute-start(f32[1032,256]{1,0:T(8,128)S(1)} %select_maximum_fusion.refs_0_), channel_id=1, source_target_pairs={{16,17},{17,18},{18,19},{19,16},{20,21},{21,22},{22,23},{23,20},{2... | collective-permute-start | bytes 3170312 | tf_op jit(solution)/shard_map/ppermute | solution.py:248
  4.9 25.9 %collective-permute-start.5 = (f32[1032,256]{1,0:T(8,128)S(1)}, f32[1032,256]{1,0:T(8,128)S(1)}, u32[]{:S(2)}, u32[]{:S(2)}) collective-permute-start(f32[1032,256]{1,0:T(8,128)S(1)} %select_maximum_fusion.refs_0_), channel_id=1, source_target_pairs={{0,3},{1,0},{2,1},{3,2},{4,7},{5,4},{6,5},{7,6},{8,11},{9,8},{10,9... | collective-permute-start | bytes 3170312 | tf_op jit(solution)/shard_map/ppermute | solution.py:248
  7.5 24.6 %collective-permute-start.1 = (f32[1032,256]{1,0:T(8,128)S(1)}, f32[1032,256]{1,0:T(8,128)}, u32[]{:S(2)}, u32[]{:S(2)}) collective-permute-start(f32[1032,256]{1,0:T(8,128)S(1)} %select_maximum_fusion.refs_0_), channel_id=1, source_target_pairs={{8,0},{17,1},{26,2},{12,4},{21,5},{30,6},{16,8},{25,9},{2,10},{20,... | collective-permute-start | bytes 3170312 | tf_op jit(solution)/shard_map/ppermute | solution.py:248
  7.6 37.7 %collective-permute-start = (f32[1032,256]{1,0:T(8,128)S(1)}, f32[1032,256]{1,0:T(8,128)}, u32[]{:S(2)}, u32[]{:S(2)}) collective-permute-start(f32[1032,256]{1,0:T(8,128)S(1)} %select_maximum_fusion.refs_0_), channel_id=1, source_target_pairs={{9,1},{18,2},{27,3},{13,5},{22,6},{31,7},{17,9},{26,10},{3,11},{21... | collective-permute-start | bytes 3170312 | tf_op jit(solution)/shard_map/ppermute | solution.py:248
  9.5 38.8 %collective-permute-start.2 = (f32[1032,256]{1,0:T(8,128)S(1)}, f32[1032,256]{1,0:T(8,128)}, u32[]{:S(2)}, u32[]{:S(2)}) collective-permute-start(f32[1032,256]{1,0:T(8,128)S(1)} %select_maximum_fusion.refs_0_), channel_id=1, source_target_pairs={{16,4},{25,5},{2,6},{11,7},{24,12},{1,13},{10,14},{19,15},{0,20},{... | collective-permute-start | bytes 3170312 | tf_op jit(solution)/shard_map/ppermute | solution.py:248
  29.5 27.0 %collective-permute-start.8 = (f32[1032,256]{1,0:T(8,128)S(1)}, f32[1032,256]{1,0:T(8,128)}, u32[]{:S(2)}, u32[]{:S(2)}) collective-permute-start(f32[1032,256]{1,0:T(8,128)S(1)} %collective-permute-done.6.refs_7_), channel_id=1, source_target_pairs={{16,17},{17,18},{18,19},{19,16},{20,21},{21,22},{22,23},{23,20},{1... | collective-permute-start | bytes 3170312 | tf_op jit(solution)/shard_map/ppermute | solution.py:248
  30.8 39.3 %collective-permute-start.7 = (f32[1032,256]{1,0:T(8,128)S(1)}, f32[1032,256]{1,0:T(8,128)}, u32[]{:S(2)}, u32[]{:S(2)}) collective-permute-start(f32[1032,256]{1,0:T(8,128)S(1)} %collective-permute-done.5.refs_6_), channel_id=1, source_target_pairs={{4,7},{5,4},{6,5},{7,6},{8,11},{9,8},{10,9},{11,10},{13,12},{14,13... | collective-permute-start | bytes 3170312 | tf_op jit(solution)/shard_map/ppermute | solution.py:248
  32.1 38.0 %collective-permute-start.4 = (f32[1032,256]{1,0:T(8,128)}, f32[1032,256]{1,0:T(8,128)}, u32[]{:S(2)}, u32[]{:S(2)}) collective-permute-start(f32[1032,256]{1,0:T(8,128)} %collective-permute-done.1.refs_2_), channel_id=1, source_target_pairs={{4,0},{5,1},{6,2},{0,4},{1,5},{2,6},{12,8},{13,9},{14,10},{8,12},{... | collective-permute-start | bytes 3170312 | tf_op jit(solution)/shard_map/ppermute | solution.py:248
  45.3 24.8 %collective-permute-start.3 = (f32[1032,256]{1,0:T(8,128)}, f32[1032,256]{1,0:T(8,128)}, u32[]{:S(2)}, u32[]{:S(2)}) collective-permute-start(f32[1032,256]{1,0:T(8,128)} %collective-permute-done.refs_1_), channel_id=1, source_target_pairs={{5,1},{6,2},{7,3},{13,9},{14,10},{15,11},{21,17},{22,18},{23,19},{... | collective-permute-start | bytes 3170312 | tf_op jit(solution)/shard_map/ppermute | solution.py:248

commit v5 on v4

--- a/solution.py
+++ b/solution.py
@@ -40,14 +40,18 @@
             ]
             perms.append((0, pairs))
         return perms
-    down = shift([r for r in range(8) if 1 in offsets[r] and not {1, 2, 3} <= set(offsets[r])], -1, 4)
-    up = shift([r for r in range(8) if 3 in offsets[r] and not {1, 2, 3} <= set(offsets[r])], 1, 4)
-    again_down = shift([r for r in range(8) if set(offsets[r]) in ({0, 1, 2}, {1, 2})], -1, 4)
-    again_up = shift([r for r in range(8) if set(offsets[r]) in ({2, 3}, {0, 2, 3})], 1, 4)
-    down += [((3, c), (3, c - 1)) for c in (1, 2, 3)] + [((3, 0), (6, 0))]
-    up += [((3, c), (3, c + 1)) for c in (0, 1, 2)] + [((3, 3), (0, 3))]
-    again_down += [((3, 1), (3, 0)), ((3, 2), (3, 1)), ((6, 0), (3, 3))]
-    again_up += [((3, 1), (3, 2)), ((3, 2), (3, 3)), ((0, 3), (3, 0))]
+    whole = [r for r in range(8) if {1, 2, 3} <= set(offsets[r])]
+    once, twice = {-1: [], 1: []}, {-1: [], 1: []}
+    for r in range(8):
+        for offset, step in ((1, -1), (3, 1)):
+            if offset in offsets[r] and r not in whole:
+                once[step].append(r)
+                if 2 in offsets[r]:
+                    twice[step].append(r)
+    down = shift([r for r in once[-1] if r != 0], -1, 4) + [((3, c), (3, c - 1)) for c in (1, 2, 3)] + [((3, 0), (0, 0))]
+    up = shift(once[1], 1, 4) + shift([0], -1, 4) + [((3, c), (3, c + 1)) for c in (0, 1, 2)] + [((3, 3), (1, 3))]
+    again_down = shift(twice[-1], -1, 4) + [((3, 1), (3, 0)), ((3, 2), (3, 1)), ((0, 0), (3, 3))]
+    again_up = shift(twice[1], 1, 4) + [((3, 1), (3, 2)), ((3, 2), (3, 3)), ((1, 3), (3, 0))]
     return [(0, down), (0, up), (1, again_down), (2, again_up)]
 
 

time: 81.7 us -> 73.6 us (0.901)
  the two profiles are of different devices: /device:TPU:27 before, /device:TPU:15 now
where the time goes in v5:
time: 73.6 us; the launch traced here: 72.8 us
  waiting for transfers between devices  42.1 us (57%)
  starting transfers between devices  17.5 us (24%)
  Pallas kernels  10.3 us (14%)
  other arithmetic  1.98 us (3%)
  local copies, waits for them, and re-layouts  0.86 us (1%)
    ppermute x9, waiting for transfers between devices, carry(): bufs.append(lax.ppermute(bufs[source], ('row', 'col'), flat))  42.1 us
    ppermute x9, starting transfers between devices, carry(): bufs.append(lax.ppermute(bufs[source], ('row', 'col'), flat))  17.5 us
    pallas_call x1, Pallas kernels, local(): pl.pallas_call(functools.partial(product_kernel, slots, n_row, ratio, rb,...  10.3 us
  transfers between devices with their start and end apart: 9, of which 4 were waited for; matrix products, arithmetic and copies ran while one was open for 1% of the time, Pallas kernels for 0%

profile of v5, /device:TPU:15, one launch (start us, length us, event | category | flops | bytes accessed | tf_op | source)
XLA Modules:
  0.0 72.8 jit_solution(4148372513594915556)
XLA Ops:
  0.0 0.7 convert_element_type.5
  0.7 0.1 copy.5
  0.8 0.1 reshape.3
  0.9 1.3 %select_maximum_fusion.refs_0_ = f32[1032,256]{1,0:T(8,128)S(1)} fusion(f32[1,64]{1,0:T(1,128)S(1)} %reshape.3, f32[1024,256]{1,0:T(8,128)} %param.4), kind=kLoop, calls=%fused_computation | loop fusion | flops 792576 | bytes 2105600 | tf_op jit(solution)/shard_map/concatenate | solution.py:246
  2.2 3.2 %collective-permute-start.6 = (f32[1032,256]{1,0:T(8,128)S(1)}, f32[1032,256]{1,0:T(8,128)S(1)}, u32[]{:S(2)}, u32[]{:S(2)}) collective-permute-start(f32[1032,256]{1,0:T(8,128)S(1)} %select_maximum_fusion.refs_0_), channel_id=1, source_target_pairs={{16,17},{17,18},{18,19},{19,16},{20,21},{21,22},{22,23},{23,20},{2... | collective-permute-start | bytes 3170312 | tf_op jit(solution)/shard_map/ppermute | solution.py:252
  5.4 2.1 %collective-permute-start.5 = (f32[1032,256]{1,0:T(8,128)S(1)}, f32[1032,256]{1,0:T(8,128)S(1)}, u32[]{:S(2)}, u32[]{:S(2)}) collective-permute-start(f32[1032,256]{1,0:T(8,128)S(1)} %select_maximum_fusion.refs_0_), channel_id=1, source_target_pairs={{4,7},{5,4},{6,5},{7,6},{8,11},{9,8},{10,9},{11,10},{28,31},{29,28... | collective-permute-start | bytes 3170312 | tf_op jit(solution)/shard_map/ppermute | solution.py:252
  7.5 0.3 collective-permute-start.1
  7.8 1.9 %collective-permute-start = (f32[1032,256]{1,0:T(8,128)S(1)}, f32[1032,256]{1,0:T(8,128)}, u32[]{:S(2)}, u32[]{:S(2)}) collective-permute-start(f32[1032,256]{1,0:T(8,128)S(1)} %select_maximum_fusion.refs_0_), channel_id=1, source_target_pairs={{9,1},{18,2},{27,3},{13,5},{22,6},{31,7},{17,9},{26,10},{3,11},{21... | collective-permute-start | bytes 3170312 | tf_op jit(solution)/shard_map/ppermute | solution.py:252
  9.7 1.3 %collective-permute-start.2 = (f32[1032,256]{1,0:T(8,128)S(1)}, f32[1032,256]{1,0:T(8,128)}, u32[]{:S(2)}, u32[]{:S(2)}) collective-permute-start(f32[1032,256]{1,0:T(8,128)S(1)} %select_maximum_fusion.refs_0_), channel_id=1, source_target_pairs={{16,4},{25,5},{2,6},{11,7},{24,12},{1,13},{10,14},{19,15},{0,20},{... | collective-permute-start | bytes 3170312 | tf_op jit(solution)/shard_map/ppermute | solution.py:252
  11.0 17.3 %collective-permute-done.6.refs_7_ = f32[1032,256]{1,0:T(8,128)S(1)} collective-permute-done((f32[1032,256]{1,0:T(8,128)S(1)}, f32[1032,256]{1,0:T(8,128)S(1)}, u32[]{:S(2)}, u32[]{:S(2)}) %collective-permute-start.6) | collective-permute-done | bytes 1056800 | tf_op jit(solution)/shard_map/ppermute | solution.py:252
  28.4 1.7 %collective-permute-start.8 = (f32[1032,256]{1,0:T(8,128)S(1)}, f32[1032,256]{1,0:T(8,128)}, u32[]{:S(2)}, u32[]{:S(2)}) collective-permute-start(f32[1032,256]{1,0:T(8,128)S(1)} %collective-permute-done.6.refs_7_), channel_id=1, source_target_pairs={{16,17},{17,18},{18,19},{19,16},{20,21},{21,22},{22,23},{23,20},{1... | collective-permute-start | bytes 3170312 | tf_op jit(solution)/shard_map/ppermute | solution.py:252
  30.0 11.7 %collective-permute-done.5.refs_6_ = f32[1032,256]{1,0:T(8,128)S(1)} collective-permute-done((f32[1032,256]{1,0:T(8,128)S(1)}, f32[1032,256]{1,0:T(8,128)S(1)}, u32[]{:S(2)}, u32[]{:S(2)}) %collective-permute-start.5) | collective-permute-done | bytes 1056800 | tf_op jit(solution)/shard_map/ppermute | solution.py:252
  41.7 1.7 %collective-permute-start.7 = (f32[1032,256]{1,0:T(8,128)S(1)}, f32[1032,256]{1,0:T(8,128)}, u32[]{:S(2)}, u32[]{:S(2)}) collective-permute-start(f32[1032,256]{1,0:T(8,128)S(1)} %collective-permute-done.5.refs_6_), channel_id=1, source_target_pairs={{4,7},{5,4},{6,5},{7,6},{8,11},{9,8},{10,9},{11,10},{13,12},{14,13... | collective-permute-start | bytes 3170312 | tf_op jit(solution)/shard_map/ppermute | solution.py:252
  43.4 12.2 %collective-permute-done.1.refs_2_ = f32[1032,256]{1,0:T(8,128)} collective-permute-done((f32[1032,256]{1,0:T(8,128)S(1)}, f32[1032,256]{1,0:T(8,128)}, u32[]{:S(2)}, u32[]{:S(2)}) %collective-permute-start.1) | collective-permute-done | bytes 1056800 | tf_op jit(solution)/shard_map/ppermute | solution.py:252
  55.5 2.4 %collective-permute-start.4 = (f32[1032,256]{1,0:T(8,128)}, f32[1032,256]{1,0:T(8,128)}, u32[]{:S(2)}, u32[]{:S(2)}) collective-permute-start(f32[1032,256]{1,0:T(8,128)} %collective-permute-done.1.refs_2_), channel_id=1, source_target_pairs={{4,0},{5,1},{6,2},{0,4},{1,5},{2,6},{12,8},{13,9},{14,10},{8,12},{... | collective-permute-start | bytes 3170312 | tf_op jit(solution)/shard_map/ppermute | solution.py:252
  57.9 0.0 collective-permute-done.refs_1_
  57.9 3.0 %collective-permute-start.3 = (f32[1032,256]{1,0:T(8,128)}, f32[1032,256]{1,0:T(8,128)}, u32[]{:S(2)}, u32[]{:S(2)}) collective-permute-start(f32[1032,256]{1,0:T(8,128)} %collective-permute-done.refs_1_), channel_id=1, source_target_pairs={{5,1},{6,2},{7,3},{13,9},{14,10},{15,11},{21,17},{22,18},{23,19},{... | collective-permute-start | bytes 3170312 | tf_op jit(solution)/shard_map/ppermute | solution.py:252
  60.9 0.7 dynamic-slice_bitcast_fusion.info_ref
  61.6 0.0 collective-permute-done.2.refs_3_
  61.6 0.0 collective-permute-done.8.refs_9_
  61.6 0.0 collective-permute-done.7.refs_8_
  61.6 0.0 collective-permute-done.4.refs_5_
  61.6 0.9 %collective-permute-done.3.refs_4_ = f32[1032,256]{1,0:T(8,128)} collective-permute-done((f32[1032,256]{1,0:T(8,128)}, f32[1032,256]{1,0:T(8,128)}, u32[]{:S(2)}, u32[]{:S(2)}) %collective-permute-start.3) | collective-permute-done | bytes 1056800 | tf_op jit(solution)/shard_map/ppermute | solution.py:252
  62.5 10.3 %shard_map.37 = f32[1024,2048]{1,0:T(8,128)} custom-call(s32[10]{0:T(128)S(1)} %dynamic-slice_bitcast_fusion.info_ref, f32[1032,256]{1,0:T(8,128)S(1)} %select_maximum_fusion.refs_0_, f32[1032,256]{1,0:T(8,128)} %collective-permute-done.refs_1_, f32[1032,256]{1,0:T(8,128)} %collective-permute-done.1.refs_2_, f32[1032,256]{1,0:T(8,128)} %collective-permute-done.2.refs_3_, ...), custom_call_target="tpu_custom_call" | custom-call | flops 1000000000 | bytes 20971520 | tf_op jit(solution)/shard_map/pallas_call | solution.py:261
Async XLA Ops:
  2.2 26.2 %collective-permute-start.6 = (f32[1032,256]{1,0:T(8,128)S(1)}, f32[1032,256]{1,0:T(8,128)S(1)}, u32[]{:S(2)}, u32[]{:S(2)}) collective-permute-start(f32[1032,256]{1,0:T(8,128)S(1)} %select_maximum_fusion.refs_0_), channel_id=1, source_target_pairs={{16,17},{17,18},{18,19},{19,16},{20,21},{21,22},{22,23},{23,20},{2... | collective-permute-start | bytes 3170312 | tf_op jit(solution)/shard_map/ppermute | solution.py:252
  5.4 36.3 %collective-permute-start.5 = (f32[1032,256]{1,0:T(8,128)S(1)}, f32[1032,256]{1,0:T(8,128)S(1)}, u32[]{:S(2)}, u32[]{:S(2)}) collective-permute-start(f32[1032,256]{1,0:T(8,128)S(1)} %select_maximum_fusion.refs_0_), channel_id=1, source_target_pairs={{4,7},{5,4},{6,5},{7,6},{8,11},{9,8},{10,9},{11,10},{28,31},{29,28... | collective-permute-start | bytes 3170312 | tf_op jit(solution)/shard_map/ppermute | solution.py:252
  7.5 48.1 %collective-permute-start.1 = (f32[1032,256]{1,0:T(8,128)S(1)}, f32[1032,256]{1,0:T(8,128)}, u32[]{:S(2)}, u32[]{:S(2)}) collective-permute-start(f32[1032,256]{1,0:T(8,128)S(1)} %select_maximum_fusion.refs_0_), channel_id=1, source_target_pairs={{8,0},{17,1},{26,2},{12,4},{21,5},{30,6},{16,8},{25,9},{2,10},{20,... | collective-permute-start | bytes 3170312 | tf_op jit(solution)/shard_map/ppermute | solution.py:252
  7.8 50.1 %collective-permute-start = (f32[1032,256]{1,0:T(8,128)S(1)}, f32[1032,256]{1,0:T(8,128)}, u32[]{:S(2)}, u32[]{:S(2)}) collective-permute-start(f32[1032,256]{1,0:T(8,128)S(1)} %select_maximum_fusion.refs_0_), channel_id=1, source_target_pairs={{9,1},{18,2},{27,3},{13,5},{22,6},{31,7},{17,9},{26,10},{3,11},{21... | collective-permute-start | bytes 3170312 | tf_op jit(solution)/shard_map/ppermute | solution.py:252
  9.7 51.9 %collective-permute-start.2 = (f32[1032,256]{1,0:T(8,128)S(1)}, f32[1032,256]{1,0:T(8,128)}, u32[]{:S(2)}, u32[]{:S(2)}) collective-permute-start(f32[1032,256]{1,0:T(8,128)S(1)} %select_maximum_fusion.refs_0_), channel_id=1, source_target_pairs={{16,4},{25,5},{2,6},{11,7},{24,12},{1,13},{10,14},{19,15},{0,20},{... | collective-permute-start | bytes 3170312 | tf_op jit(solution)/shard_map/ppermute | solution.py:252
  28.4 33.2 %collective-permute-start.8 = (f32[1032,256]{1,0:T(8,128)S(1)}, f32[1032,256]{1,0:T(8,128)}, u32[]{:S(2)}, u32[]{:S(2)}) collective-permute-start(f32[1032,256]{1,0:T(8,128)S(1)} %collective-permute-done.6.refs_7_), channel_id=1, source_target_pairs={{16,17},{17,18},{18,19},{19,16},{20,21},{21,22},{22,23},{23,20},{1... | collective-permute-start | bytes 3170312 | tf_op jit(solution)/shard_map/ppermute | solution.py:252
  41.7 19.9 %collective-permute-start.7 = (f32[1032,256]{1,0:T(8,128)S(1)}, f32[1032,256]{1,0:T(8,128)}, u32[]{:S(2)}, u32[]{:S(2)}) collective-permute-start(f32[1032,256]{1,0:T(8,128)S(1)} %collective-permute-done.5.refs_6_), channel_id=1, source_target_pairs={{4,7},{5,4},{6,5},{7,6},{8,11},{9,8},{10,9},{11,10},{13,12},{14,13... | collective-permute-start | bytes 3170312 | tf_op jit(solution)/shard_map/ppermute | solution.py:252
  55.5 6.0 %collective-permute-start.4 = (f32[1032,256]{1,0:T(8,128)}, f32[1032,256]{1,0:T(8,128)}, u32[]{:S(2)}, u32[]{:S(2)}) collective-permute-start(f32[1032,256]{1,0:T(8,128)} %collective-permute-done.1.refs_2_), channel_id=1, source_target_pairs={{4,0},{5,1},{6,2},{0,4},{1,5},{2,6},{12,8},{13,9},{14,10},{8,12},{... | collective-permute-start | bytes 3170312 | tf_op jit(solution)/shard_map/ppermute | solution.py:252
  57.9 4.6 %collective-permute-start.3 = (f32[1032,256]{1,0:T(8,128)}, f32[1032,256]{1,0:T(8,128)}, u32[]{:S(2)}, u32[]{:S(2)}) collective-permute-start(f32[1032,256]{1,0:T(8,128)} %collective-permute-done.refs_1_), channel_id=1, source_target_pairs={{5,1},{6,2},{7,3},{13,9},{14,10},{15,11},{21,17},{22,18},{23,19},{... | collective-permute-start | bytes 3170312 | tf_op jit(solution)/shard_map/ppermute | solution.py:252
